TPU v7x, 256 devices: a whole 4x4x8 slice. The times are simulated.
256 devices in a mesh: seq: 64 (over x, z, core), tp: 4 (over y).
Axes of the slice: x: 4, y: 4, z: 8, core: 2. Of those that a mesh axis runs over, the one named last changes fastest.
Arguments:
- hidden_in: bfloat16 [256, 2048], P('seq'), may hold values from -6 to 6
- query_weight: bfloat16 [2048, 2048], P(None, 'tp'), may hold values from -0.125 to 0.125
- key_weight: bfloat16 [2048, 2048], P(None, 'tp'), may hold values from -0.125 to 0.125
- value_weight: bfloat16 [2048, 2048], P(None, 'tp'), may hold values from -0.125 to 0.125
- out_weight: bfloat16 [2048, 2048], P('tp'), may hold values from -0.125 to 0.125
- query_gain: float32 [2048], P('tp'), may hold values from 0.5 to 1.5
- key_gain: float32 [2048], P('tp'), may hold values from 0.5 to 1.5
- post_gain: float32 [2048], P('tp'), may hold values from 0.5 to 1.5
- key_cache: bfloat16 [4, 8192, 2048], P(None, 'seq', 'tp'), may hold values from -110 to 110
- value_cache: bfloat16 [4, 8192, 2048], P(None, 'seq', 'tp'), may hold values from -6 to 6
- cache_lengths: int32 [4], replicated, may hold values from 1024 to 8128
- parents: int32 [4, 64], replicated, may hold values from -1 to 62, as said below
- accepted_leaf: int32 [4], replicated, may hold values from 0 to 63
Outputs:
- hidden_out: bfloat16 [256, 2048], P('seq', 'tp')
- new_key_cache: bfloat16 [4, 8192, 2048], P(None, 'seq', 'tp')
- new_value_cache: bfloat16 [4, 8192, 2048], P(None, 'seq', 'tp')
Inputs may be any that keep to these rules, and one draw needn't show every extreme that they name: parents[r, 0] = -1; for i >= 1, parents[r, i] lies in max(0, i - 3) to i - 1; parents[r, 63] = 62.
All inputs are finite; a program needn't handle non-finite values.
Results may differ from a plain program's by a relative error of at most 0.019.
Values may be sent and summed in bfloat16 or wider, within the bound.
A program may use at most 128 MiB of HBM per device.

v0:
```python
import math

import jax
import jax.numpy as jnp
from jax import lax
from jax.sharding import PartitionSpec as P

HEAD_DIM = 128


EPS = 1e-06
THETA = 500000.0
NEG = -1e30


def joined_2(x, axis, combine):
    everything = jax.tree.map(lambda part: lax.all_gather(part, axis), x)
    initial = jax.tree.map(lambda part: part[0], everything)

    def step(k, so_far):
        return combine(so_far, jax.tree.map(lambda part: part[k], everything))

    return lax.fori_loop(1, lax.axis_size(axis), step, initial)


def ancestry(parents):
    number = parents.shape[-1]
    columns = jnp.arange(number, dtype=jnp.int32)
    single = (parents[:, :, None] == columns[None, None, :]).astype(jnp.float32)
    ancestors = jnp.eye(number, dtype=jnp.float32)[None] + single
    for repeat in range(max(1, (number - 1).bit_length())):
        ancestors = jnp.minimum(
            jnp.einsum("rij,rjk->rik", ancestors, ancestors, precision=lax.Precision.HIGHEST), 1.0
        )
    tree_depth = jnp.sum(ancestors, axis=-1) - 1.0
    return (ancestors, tree_depth)


def rotary(values, positions):
    half_dim = values.shape[-1] // 2
    freqs = THETA ** (-2.0 * jnp.arange(half_dim, dtype=jnp.float32) / values.shape[-1])
    angles = positions[:, None, None] * freqs[None, None, :]
    cosine = jnp.cos(angles)
    sine = jnp.sin(angles)
    first = values[..., :half_dim]
    second = values[..., half_dim:]
    return jnp.concatenate(
        [first * cosine - second * sine, second * cosine + first * sine], axis=-1
    )


def prepare(raw, square_sum, gain, positions, width_all):
    scaled = raw * lax.rsqrt(square_sum / width_all + EPS)[:, None] * gain[None, :]
    rows_here = raw.shape[0]
    heads_here = raw.shape[1] // HEAD_DIM
    turned = rotary(scaled.reshape(rows_here, heads_here, HEAD_DIM), positions)
    return turned.reshape(rows_here, heads_here * HEAD_DIM).astype(jnp.bfloat16)


def join_partials(first, second):
    peak_first, total_first, out_first = first
    peak_second, total_second, out_second = second
    highest = jnp.maximum(peak_first, peak_second)
    scale_first = jnp.exp(peak_first - highest)
    scale_second = jnp.exp(peak_second - highest)
    rows_here, heads_here = highest.shape
    joined = (
        out_first.reshape(rows_here, heads_here, -1) * scale_first[..., None]
        + out_second.reshape(rows_here, heads_here, -1) * scale_second[..., None]
    )
    return (
        highest,
        total_first * scale_first + total_second * scale_second,
        joined.reshape(out_first.shape),
    )


def body(
    hidden_in,
    query_weight,
    key_weight,
    value_weight,
    out_weight,
    query_gain,
    key_gain,
    post_gain,
    key_cache,
    value_cache,
    cache_lengths,
    parents,
    accepted_leaf,
):
    requests, block, local_width = key_cache.shape
    draft = parents.shape[1]
    tokens = requests * draft
    own_rows = hidden_in.shape[0]
    model_width = hidden_in.shape[1]
    heads_here = local_width // HEAD_DIM
    full_width = local_width * lax.axis_size("tp")
    seq_index = lax.axis_index("seq")
    tp_index = lax.axis_index("tp")
    row_start = seq_index * own_rows
    ancestors, tree_depth = ancestry(parents)
    positions = (cache_lengths[:, None].astype(jnp.float32) + tree_depth).reshape(tokens)
    piece = lax.all_gather(hidden_in, "seq", axis=0, tiled=True)
    raw = jnp.concatenate(
        [
            jnp.dot(piece, query_weight, preferred_element_type=jnp.float32),
            jnp.dot(piece, key_weight, preferred_element_type=jnp.float32),
            jnp.dot(piece, value_weight, preferred_element_type=jnp.float32),
        ],
        axis=1,
    )
    query_raw = raw[:, :local_width]
    key_raw = raw[:, local_width : 2 * local_width]
    value_raw = raw[:, 2 * local_width :]
    query_square, key_square = lax.psum(
        (jnp.sum(query_raw * query_raw, axis=1), jnp.sum(key_raw * key_raw, axis=1)), "tp"
    )
    queries = prepare(query_raw, query_square, query_gain, positions, full_width)
    keys = prepare(key_raw, key_square, key_gain, positions, full_width)
    values = value_raw.astype(jnp.bfloat16)
    factor = 1.0 / math.sqrt(HEAD_DIM)
    query_blocks = queries.reshape(requests, draft, heads_here, HEAD_DIM)
    cache_keys = key_cache.reshape(requests, block, heads_here, HEAD_DIM)
    cache_values = value_cache.reshape(requests, block, heads_here, HEAD_DIM)
    places = seq_index * block + jnp.arange(block, dtype=jnp.int32)
    cache_scores = (
        jnp.einsum("rihd,rlhd->rihl", query_blocks, cache_keys, preferred_element_type=jnp.float32)
        * factor
    )
    visible = (places[None, :] < cache_lengths[:, None])[:, None, None, :]
    cache_scores = jnp.where(visible, cache_scores, NEG)
    cache_peak = jnp.max(cache_scores, axis=-1)
    cache_weights = jnp.where(visible, jnp.exp(cache_scores - cache_peak[..., None]), 0.0)
    cache_total = jnp.sum(cache_weights, axis=-1).reshape(tokens, heads_here)
    cache_out = jnp.einsum(
        "rihl,rlhd->rihd",
        cache_weights,
        cache_values.astype(jnp.float32),
        precision=lax.Precision.HIGHEST,
    ).reshape(tokens, local_width)
    cache_peak = cache_peak.reshape(tokens, heads_here)
    request_now = row_start // draft
    own_queries_all = lax.dynamic_slice_in_dim(queries, row_start, own_rows).reshape(
        own_rows, heads_here, HEAD_DIM
    )
    request_keys = lax.dynamic_index_in_dim(
        keys.reshape(requests, draft, local_width), request_now, 0, keepdims=False
    ).reshape(draft, heads_here, HEAD_DIM)
    request_values = lax.dynamic_index_in_dim(
        values.reshape(requests, draft, local_width), request_now, 0, keepdims=False
    ).reshape(draft, heads_here, HEAD_DIM)
    tree_rows = lax.dynamic_slice_in_dim(ancestors.reshape(tokens, draft), row_start, own_rows)
    draft_scores = (
        jnp.einsum(
            "ihd,jhd->ihj", own_queries_all, request_keys, preferred_element_type=jnp.float32
        )
        * factor
    )
    tree_mask = (tree_rows > 0.5)[:, None, :]
    draft_scores = jnp.where(tree_mask, draft_scores, NEG)
    draft_peak = jnp.max(draft_scores, axis=-1)
    draft_weights = jnp.where(tree_mask, jnp.exp(draft_scores - draft_peak[..., None]), 0.0)
    draft_total = jnp.sum(draft_weights, axis=-1)
    draft_out = jnp.einsum(
        "ihj,jhd->ihd",
        draft_weights,
        request_values.astype(jnp.float32),
        precision=lax.Precision.HIGHEST,
    ).reshape(own_rows, local_width)
    merged = joined_2((cache_peak, cache_total, cache_out), "seq", join_partials)
    mine = tuple((lax.dynamic_slice_in_dim(member, row_start, own_rows) for member in merged))
    highest, denominator, summed = join_partials(mine, (draft_peak, draft_total, draft_out))
    attention = (
        (summed.reshape(own_rows, heads_here, HEAD_DIM) / denominator[..., None])
        .reshape(own_rows, local_width)
        .astype(jnp.bfloat16)
    )
    projected = jnp.dot(attention, out_weight, preferred_element_type=jnp.float32)
    feature_count = model_width // lax.axis_size("tp")
    summed_heads = lax.psum(projected, "tp")
    power = jnp.sum(summed_heads * summed_heads, axis=1)
    own_columns = lax.dynamic_slice_in_dim(summed_heads, tp_index * feature_count, feature_count, 1)
    normed = own_columns * lax.rsqrt(power / model_width + EPS)[:, None] * post_gain[None, :]
    residual_columns = lax.dynamic_slice_in_dim(
        hidden_in, tp_index * feature_count, feature_count, 1
    ).astype(jnp.float32)
    hidden_out = (residual_columns + normed).astype(jnp.bfloat16)
    leaf_onehot = (accepted_leaf[:, None] == jnp.arange(draft, dtype=jnp.int32)[None, :]).astype(
        jnp.float32
    )
    on_path = jnp.einsum("ri,rij->rj", leaf_onehot, ancestors, precision=lax.Precision.HIGHEST)
    target = cache_lengths[:, None] + tree_depth.astype(jnp.int32)
    placing = (places[None, :, None] == target[:, None, :]) & (on_path[:, None, :] > 0.5)
    written = jnp.any(placing, axis=-1)[..., None]
    placing_half = placing.astype(jnp.bfloat16)
    fresh_keys = jnp.einsum(
        "rpj,rjw->rpw",
        placing_half,
        keys.reshape(requests, draft, local_width),
        preferred_element_type=jnp.float32,
    ).astype(jnp.bfloat16)
    fresh_values = jnp.einsum(
        "rpj,rjw->rpw",
        placing_half,
        values.reshape(requests, draft, local_width),
        preferred_element_type=jnp.float32,
    ).astype(jnp.bfloat16)
    new_key_cache = jnp.where(written, fresh_keys, key_cache)
    new_value_cache = jnp.where(written, fresh_values, value_cache)
    return (hidden_out, new_key_cache, new_value_cache)


def solution(mesh):
    return jax.shard_map(
        body,
        mesh=mesh,
        in_specs=(
            P("seq", None),
            P(None, "tp"),
            P(None, "tp"),
            P(None, "tp"),
            P("tp", None),
            P("tp"),
            P("tp"),
            P("tp"),
            P(None, "seq", "tp"),
            P(None, "seq", "tp"),
            P(),
            P(),
            P(),
        ),
        out_specs=(P("seq", "tp"), P(None, "seq", "tp"), P(None, "seq", "tp")),
        check_vma=False,
    )
```

profile of v0, /device:TPU:1, one launch (start us, length us, event | category | flops | bytes accessed | tf_op | source)
XLA Modules:
  0.0 471.1 jit_solution(13318958439840656037)
XLA Ops:
  12.0 79.4 %all-gather.6.cloned.1.call-done = bf16[64,4,2048]{2,1,0:T(4,128)(2,1)} async-done(((bf16[1,4,2048]{2,1,0:T(4,128)(2,1)}), bf16[64,4,2048]{2,1,0:T(4,128)(2,1)}) %all-gather.6.cloned.1.call-update) | async-done | bytes 1048592 | tf_op jit(solution)/shard_map/all_gather | solution.py:105
  92.8 2.1 multiply_reduce_fusion
  94.9 2.1 multiply_reduce_fusion.1
  97.0 8.6 %all-reduce = (f32[256]{0:T(256)S(1)}, f32[256]{0:T(256)S(1)}) all-reduce(f32[256]{0:T(256)} %get-tuple-element.217, f32[256]{0:T(256)} %get-tuple-element.219), channel_id=1, replica_groups=mesh['seq'=64,'tp'=4] {'tp'}, use_global_device_ids=true, to_apply=%region_1.0 | all-reduce | flops 512 | bytes 4096 | tf_op jit(solution)/shard_map/psum | solution.py:117
  114.4 2.6 convolution_convert_fusion.2
  122.8 45.0 %all_gather.14 = f32[64,256,4]{1,2,0:T(4,128)S(1)} all-gather(f32[1,256,4]{1,2,0:T(4,128)S(1)} %all_gather_reshape.10), channel_id=1, replica_groups=mesh['seq'=64,'tp'=4] {'seq'}, dimensions={0}, use_global_device_ids=true | all-gather | bytes 266240 | tf_op jit(solution)/shard_map/all_gather | solution.py:17
  167.7 42.6 %all_gather.13 = f32[64,256,4]{1,2,0:T(4,128)S(1)} all-gather(f32[1,256,4]{1,2,0:T(4,128)S(1)} %all_gather_reshape.9), channel_id=1, replica_groups=mesh['seq'=64,'tp'=4] {'seq'}, dimensions={0}, use_global_device_ids=true | all-gather | bytes 266240 | tf_op jit(solution)/shard_map/all_gather | solution.py:17
  213.3 2.2 fusion.4
  215.6 1.9 fusion.3
  217.5 35.1 %all-gather.4.cloned.1.call-done = f32[64,256,512]{2,1,0:T(8,128)} async-done(((f32[1,256,512]{2,1,0:T(8,128)}), f32[64,256,512]{2,1,0:T(8,128)}) %all-gather.4.cloned.1.call-update) | async-done | bytes 33554448 | tf_op jit(solution)/shard_map/all_gather | solution.py:17
  253.7 193.7 %while.19 = (s32[]{:T(128)}, f32[256,4]{0,1:T(4,128)S(1)}, f32[256,4]{0,1:T(4,128)S(1)}, f32[256,512]{1,0:T(8,128)S(1)}, f32[64,256,4]{1,2,0:T(4,128)}, /*index=...) while((s32[]{:T(128)}, f32[256,4]{0,1:T(4,128)S(1)}, ...), condition=%wide.region_6.7_spmd, body=%wide.region_5.6_spmd.sunk | while | flops 399365 | bytes 3727503 | solution.py:23
  255.3 1.4 fusion.87
  258.4 1.4 fusion.87
  261.5 1.4 fusion.87
  264.6 1.4 fusion.87
  267.6 1.4 fusion.87
  270.7 1.4 fusion.87
  273.8 1.4 fusion.87
  276.8 1.4 fusion.87
  279.9 1.4 fusion.87
  283.0 1.4 fusion.87
  286.1 1.4 fusion.87
  289.1 1.4 fusion.87
  292.2 1.4 fusion.87
  295.3 1.4 fusion.87
  298.3 1.4 fusion.87
  301.4 1.4 fusion.87
  304.5 1.4 fusion.87
  307.5 1.4 fusion.87
  310.6 1.4 fusion.87
  313.7 1.4 fusion.87
  316.8 1.4 fusion.87
  319.8 1.4 fusion.87
  322.9 1.4 fusion.87
  326.0 1.4 fusion.87
  329.0 1.4 fusion.87
  332.1 1.4 fusion.87
  335.2 1.4 fusion.87
  338.2 1.4 fusion.87
  341.3 1.4 fusion.87
  353.7 1.4 fusion.87
  363.0 1.4 fusion.87
  366.0 1.4 fusion.87
  375.3 1.4 fusion.87
  399.9 1.4 fusion.87
  421.4 1.4 fusion.87
  447.7 2.0 fusion.59
  449.7 13.1 %psum.23 = f32[4,2048]{1,0:T(4,128)S(1)} all-reduce(f32[4,2048]{1,0:T(4,128)S(1)} %fusion.59), channel_id=1, replica_groups=mesh['seq'=64,'tp'=4] {'tp'}, use_global_device_ids=true, to_apply=%region_11.12 | all-reduce | flops 8192 | bytes 65536 | tf_op jit(solution)/shard_map/psum | solution.py:182
  (460 shorter events, 169.2 us)
Async XLA Ops:
  7.2 85.6 %copy-start = (bf16[2048,512]{1,0:T(8,128)(2,1)S(1)}, bf16[2048,512]{1,0:T(8,128)(2,1)}, u32[]{:S(2)}) copy-start(bf16[2048,512]{1,0:T(8,128)(2,1)} %param.17) | copy-start | bytes 6291460
  7.2 4.2 copy-start.23
  7.2 84.2 %all-gather.6.cloned.1.call-start = ((), (), s32[]{:S(2)}) async-start(), calls=%async_computation.1 | async-start | bytes 1064960 | tf_op jit(solution)/shard_map/all_gather | solution.py:105
  7.9 244.6 %all-gather.4.cloned.1.call-start = ((), (), s32[]{:S(2)}) async-start(), calls=%async_computation | async-start | bytes 34078720 | tf_op jit(solution)/shard_map/all_gather | solution.py:17
  11.4 83.5 %copy-start.15 = (s32[128]{0:T(128)}, s32[128]{0:T(128)S(1)}, u32[]{:S(2)}) copy-start(s32[128]{0:T(128)S(1)} %iota_add_fusion) | copy-start | bytes 1540
  11.5 97.6 %copy-start.21 = (pred[4,128]{1,0:T(4,128)(4,1)}, pred[4,128]{1,0:T(4,128)(4,1)S(1)}, u32[]{:S(2)}) copy-start(pred[4,128]{1,0:T(4,128)(4,1)S(1)} %broadcast_compare_fusion.1) | copy-start | bytes 1540
  92.8 4.2 copy-start.5
  92.8 2.2 copy-start.25
  94.9 11.2 %copy-start.19 = (f32[512]{0:T(512)S(1)}, f32[512]{0:T(512)}, u32[]{:S(2)}) copy-start(f32[512]{0:T(512)} %param.20) | copy-start | bytes 6148
  107.5 1.0 copy-start.7
  107.8 1.3 copy-start.1
  109.1 0.8 copy-start.3
  109.1 2.8 copy-start.26
  109.1 3.0 copy-start.24
  109.1 3.1 copy-start.16
  112.2 4.9 %copy-start.13 = (pred[4,64]{1,0:T(4,128)(4,1)}, pred[4,64]{1,0:T(4,128)(4,1)S(1)}, u32[]{:S(2)}) copy-start(pred[4,64]{1,0:T(4,128)(4,1)S(1)} %broadcast_compare_fusion) | copy-start | bytes 772
  113.8 4.0 copy-start.6
  113.8 4.0 copy-start.18
  113.8 4.0 copy-start.20
  117.1 0.7 copy-start.9
  118.5 3.2 copy-start.4
  118.6 94.7 %copy-start.2 = (bf16[4,128,512]{2,1,0:T(8,128)(2,1)S(1)}, bf16[4,128,512]{2,1,0:T(8,128)(2,1)}, u32[]{:S(2)}) copy-start(bf16[4,128,512]{2,1,0:T(8,128)(2,1)} %param.24) | copy-start | bytes 1572868
  118.6 94.7 %copy-start.14 = (pred[4,64]{1,0:T(4,128)(4,1)S(1)}, pred[4,64]{1,0:T(4,128)(4,1)}, u32[]{:S(2)}) copy-start(pred[4,64]{1,0:T(4,128)(4,1)} %copy-done.13) | copy-start | bytes 772
  122.7 92.9 %copy-start.8 = (bf16[4,128,512]{2,1,0:T(8,128)(2,1)S(1)}, bf16[4,128,512]{2,1,0:T(8,128)(2,1)}, u32[]{:S(2)}) copy-start(bf16[4,128,512]{2,1,0:T(8,128)(2,1)} %param.23) | copy-start | bytes 1572868
  167.7 45.5 %copy-start.10 = (f32[64,256,4]{1,2,0:T(4,128)}, f32[64,256,4]{1,2,0:T(4,128)S(1)}, u32[]{:S(2)}) copy-start(f32[64,256,4]{1,2,0:T(4,128)S(1)} %all_gather.14) | copy-start | bytes 786436
  210.3 2.9 copy-start.11
  253.6 193.8 %copy-start.12 = (bf16[64,4,128]{2,1,0:T(4,128)(2,1)S(1)}, bf16[64,4,128]{2,1,0:T(4,128)(2,1)}, u32[]{:S(2)}) copy-start(bf16[64,4,128]{2,1,0:T(4,128)(2,1)} %reshape.240) | copy-start | bytes 196612
  253.6 193.8 %copy-start.17 = (pred[4,64]{1,0:T(4,128)(4,1)S(1)}, pred[4,64]{1,0:T(4,128)(4,1)}, u32[]{:S(2)}) copy-start(pred[4,64]{1,0:T(4,128)(4,1)} %fusion.43) | copy-start | bytes 772
  447.4 15.6 %copy-start.22 = (f32[512]{0:T(512)S(1)}, f32[512]{0:T(512)}, u32[]{:S(2)}) copy-start(f32[512]{0:T(512)} %param.22) | copy-start | bytes 6148
Sparse Core Ops, SparseCore 0:
  10.8 80.5 all-gather.5
  111.4 141.1 all-gather.3
where the time goes:
time: 478 us; the launch traced here: 471 us
  other arithmetic  141 us (29%)
  waiting for transfers between devices  115 us (24%)
  blocking collectives  109 us (23%)
  local copies, waits for them, and re-layouts  71 us (15%)
  matrix products  17.9 us (4%)
  between operations  14.6 us (3%)
    all_gather x2, blocking collectives, joined_2(): everything = jax.tree.map(lambda part: lax.all_gather(part, axis), x)  87.5 us
    add x63, other arithmetic, join_partials(): out_first.reshape(rows_here, heads_here, -1) * scale_first[..., None]  87 us
    all_gather x1, waiting for transfers between devices, body(): piece = lax.all_gather(hidden_in, 'seq', axis=0, tiled=True)  79.4 us
    add x64, other arithmetic, join_partials(): total_first * scale_first + total_second * scale_second  45 us
    all_gather x1, waiting for transfers between devices, joined_2(): everything = jax.tree.map(lambda part: lax.all_gather(part, axis), x)  35.1 us
    mul x63, local copies, waits for them, and re-layouts, join_partials(): out_first.reshape(rows_here, heads_here, -1) * scale_first[..., None]  21.1 us
    mul x63, local copies, waits for them, and re-layouts, join_partials(): out_second.reshape(rows_here, heads_here, -1) * scale_second[..., None]  21.1 us
    psum x1, blocking collectives, body(): summed_heads = lax.psum(projected, 'tp')  13.1 us
  transfers between devices with their start and end apart: 2, of which 2 were waited for; matrix products, arithmetic and copies ran while one was open for 5% of the time, Pallas kernels for 0%

commit v1 on v0

v1 whole, which is shorter than its diff:
```python
import math

import jax
import jax.numpy as jnp
import numpy as np
from jax import lax
from jax.experimental import pallas as pl
from jax.experimental.pallas import tpu as pltpu
from jax.sharding import PartitionSpec as P

HEAD_DIM = 128
EPS = 1e-06
THETA = 500000.0
NEG = -1e30
NX, NZ, NC, NT = 4, 8, 2, 4
HEADS = 4
OWN = 4
ROWS = HEADS * OWN
DRAFT = 64
REQ = 4
WIDTH = HEADS * HEAD_DIM
BLOCK = 128
MESH = pl.DeviceIdType.MESH
F32 = jnp.float32
BF16 = jnp.bfloat16
PLANES = (0, 1, 3, 2)
FAR_Z = (4, 3, 5, 2, 6, 1, 7, 0)


def far_first():
    hops = lambda a, b: min(a, NX - a) + min(b, NZ - b)
    pairs = [(a, b) for a in range(NX) for b in range(NZ) if (a, b) != (0, 0)]
    return sorted(pairs, key=lambda pair: -hops(*pair))


def iota(shape, dim):
    return lax.broadcasted_iota(jnp.int32, shape, dim)


def nt_dot(a, b):
    return lax.dot_general(a, b, (((1,), (1,)), ((), ())), preferred_element_type=F32)


def dot(a, b):
    return jnp.dot(a, b, preferred_element_type=F32)


def kernel(
    hid, wq, wk, wv, wo, qg, kg, pg, kc, vc, lens, par, leaf, freq,
    out_h, out_k, out_v,
    hid_s, wq_s, wk_s, wv_s, wo_s, qg_s, kg_s, pg_s, par_s, freq_s, lens_s, leaf_s,
    kfull, vfull, anc_s, sq_send, sq_recv, q_own, k_own, v_own, qbuf, kbuf, vbuf,
    o_st, s_st, obuf, sbuf, att_s, pr_s, pr_send, pr_recv, nk_s, nv_s, oh_s,
    lsem, swap_sem, sq_sem, q_sem, q_send, z_sem, x_sem, c_sem, o_sem, s_sem, p_sem, out_sem,
):
    seq = lax.axis_index("seq")
    tp = lax.axis_index("tp")
    core = lax.rem(seq, NC)
    zz = lax.rem(seq // NC, NZ)
    xx = seq // (NC * NZ)

    def at(dx, dz):
        return ((lax.rem(xx + dx, NX) * NZ + lax.rem(zz + dz, NZ)) * NC + core, tp)

    partner = (seq + 1 - 2 * core, tp)
    y_peers = [(seq, lax.rem(tp + d, NT)) for d in range(1, NT)]
    plane_peers = [at(a, b) for a, b in far_first()]

    barrier = pltpu.get_barrier_semaphore()
    for peer in plane_peers + y_peers + [partner]:
        pl.semaphore_signal(barrier, inc=1, device_id=peer, device_id_type=MESH)

    pairs = [
        (par, par_s), (lens, lens_s), (freq, freq_s), (hid, hid_s), (wq, wq_s), (wk, wk_s), (wv, wv_s),
        (qg, qg_s), (kg, kg_s), (pg, pg_s), (leaf, leaf_s),
        (kc, kfull.at[:, pl.ds(core * BLOCK, BLOCK), :]),
        (vc, vfull.at[:, pl.ds(core * BLOCK, BLOCK), :]),
        (wo, wo_s),
    ]
    local = [pltpu.make_async_copy(a, b, lsem.at[i]) for i, (a, b) in enumerate(pairs)]
    for copy in local:
        copy.start()
    (c_par, c_lens, c_freq, c_hid, c_wq, c_wk, c_wv, c_qg, c_kg, c_pg, c_leaf, c_kc, c_vc, c_wo) = local

    def remote(src, dst, send, recv, peer):
        copy = pltpu.make_async_remote_copy(
            src_ref=src, dst_ref=dst, send_sem=send, recv_sem=recv, device_id=peer, device_id_type=MESH
        )
        copy.start()

    def wait(ref, sem):
        pltpu.make_async_copy(ref, ref, sem).wait()

    c_par.wait()
    square = (DRAFT, DRAFT)
    eye = (iota(square, 0) == iota(square, 1)).astype(F32)
    chains = []
    for r in range(REQ):
        up = (par_s[pl.ds(r, 1), :] == iota(square, 0)).astype(F32)
        chains.append((eye + up).astype(BF16))
    for _ in range(6):
        chains = [jnp.minimum(dot(a, a), 1.0).astype(BF16) for a in chains]
    for r in range(REQ):
        anc_s[r] = chains[r]

    chunk = (ROWS, HEAD_DIM)
    row_head = (iota(chunk, 0) >> 2) & 3
    lane = iota(chunk, 1)
    row_token = (zz * NC + core) * OWN + (iota((ROWS, DRAFT), 0) & 3)
    one_hot = (iota((ROWS, DRAFT), 1) == row_token).astype(F32).astype(BF16)
    anc_rows = nt_dot(one_hot, anc_s[xx])
    depth = jnp.sum(anc_rows, axis=1, keepdims=True) - 1.0
    c_lens.wait()
    position = lens_s[xx].astype(F32) + depth
    c_freq.wait()
    angle = position * freq_s[...]
    cosine = jnp.cos(angle)
    sine = jnp.sin(angle)
    sine = jnp.where(lane < HEAD_DIM // 2, -sine, sine)

    c_hid.wait()
    h4 = hid_s[...].astype(F32)
    h8 = jnp.concatenate([h4, h4], axis=0)
    h16 = jnp.concatenate([h8, h8], axis=0).astype(BF16)

    def diagonal(wide):
        picked = wide[:, :HEAD_DIM]
        for h in range(1, HEADS):
            picked = jnp.where(row_head == h, wide[:, h * HEAD_DIM : (h + 1) * HEAD_DIM], picked)
        return picked

    def spread(gain):
        return diagonal(jnp.broadcast_to(gain, (ROWS, WIDTH)))

    c_wq.wait()
    q_wide = dot(h16, wq_s[...])
    c_wk.wait()
    k_wide = dot(h16, wk_s[...])
    q_sq = jnp.sum(q_wide * q_wide, axis=1, keepdims=True)
    k_sq = jnp.sum(k_wide * k_wide, axis=1, keepdims=True)
    lane8 = iota((8, HEAD_DIM), 1)
    sq_mine = jnp.where(lane8 < HEAD_DIM // 2, q_sq[:8], k_sq[:8])
    sq_send[...] = sq_mine
    c_wv.wait()
    v_own[...] = diagonal(dot(h16, wv_s[...])).astype(BF16)
    for copy in (c_qg, c_kg):
        copy.wait()
    q_turn = diagonal(q_wide) * spread(qg_s[...])
    k_turn = diagonal(k_wide) * spread(kg_s[...])
    q_turn = q_turn * cosine + pltpu.roll(q_turn, HEAD_DIM // 2, 1) * sine
    k_turn = k_turn * cosine + pltpu.roll(k_turn, HEAD_DIM // 2, 1) * sine

    pl.semaphore_wait(barrier, len(plane_peers) + len(y_peers) + 1)

    for i, peer in enumerate(y_peers):
        remote(sq_send, sq_recv.at[i], sq_sem.at[0], sq_sem.at[1], peer)
    mine = pl.ds(core * BLOCK, BLOCK)
    remote(kc, kfull.at[:, mine, :], swap_sem.at[0], swap_sem.at[1], partner)
    remote(vc, vfull.at[:, mine, :], swap_sem.at[2], swap_sem.at[3], partner)

    wait(sq_recv, sq_sem.at[1])
    total = sq_mine + sq_recv[0] + sq_recv[1] + sq_recv[2]
    scale = lax.rsqrt(total / (NT * WIDTH) + EPS)
    other = pltpu.roll(scale, HEAD_DIM // 2, 1)
    q_scale = jnp.where(lane8 < HEAD_DIM // 2, scale, other)
    k_scale = jnp.where(lane8 < HEAD_DIM // 2, other, scale)
    q_own[...] = (q_turn * jnp.concatenate([q_scale, q_scale], axis=0)).astype(BF16)
    k_own[...] = (k_turn * jnp.concatenate([k_scale, k_scale], axis=0)).astype(BF16)

    for peer in plane_peers:
        remote(q_own, qbuf.at[xx * NZ + zz], q_send, q_sem.at[xx], peer)
    pltpu.make_async_copy(q_own, qbuf.at[xx * NZ + zz], q_sem.at[xx]).start()
    for dz in FAR_Z[:-1]:
        remote(k_own, kbuf.at[core, xx, zz], z_sem.at[0], z_sem.at[1], at(0, dz))
        remote(v_own, vbuf.at[core, xx, zz], z_sem.at[2], z_sem.at[3], at(0, dz))
    pltpu.make_async_copy(k_own, kbuf.at[core, xx, zz], z_sem.at[1]).start()
    pltpu.make_async_copy(v_own, vbuf.at[core, xx, zz], z_sem.at[3]).start()

    factor = 1.0 / math.sqrt(HEAD_DIM)
    tall = (NZ * ROWS, NC * BLOCK)
    tall_head = (iota(tall, 0) >> 2) & 3
    place = (seq - core) * BLOCK + iota(tall, 1)
    turn = iota((NZ * ROWS, HEAD_DIM), 0) == iota((NZ * ROWS, HEAD_DIM), 1)
    c_kc.wait()
    c_vc.wait()
    wait(kfull.at[:, mine, :], swap_sem.at[1])
    wait(vfull.at[:, mine, :], swap_sem.at[3])
    for step, dx in enumerate(PLANES):
        r = lax.rem(xx + dx, NX)
        group = pl.ds(r * NZ, NZ)
        wait(qbuf.at[group], q_sem.at[r])
        queries = qbuf[group].reshape(NZ * ROWS, HEAD_DIM)
        scores = None
        for h in range(HEADS):
            part = nt_dot(queries, kfull[r, :, h * HEAD_DIM : (h + 1) * HEAD_DIM])
            scores = part if h == 0 else jnp.where(tall_head == h, part, scores)
        visible = place < lens_s[r]
        scores = jnp.where(visible, scores * factor, NEG)
        peak = jnp.max(scores, axis=1, keepdims=True)
        weights = jnp.where(visible, jnp.exp(scores - peak), 0.0)
        weight_sum = jnp.sum(weights, axis=1, keepdims=True)
        mixed = None
        for h in range(HEADS):
            masked = jnp.where(tall_head == h, weights, 0.0).astype(BF16)
            part = dot(masked, vfull[r, :, h * HEAD_DIM : (h + 1) * HEAD_DIM])
            mixed = part if h == 0 else mixed + part
        o_st[step] = mixed.astype(BF16).reshape(NZ, ROWS, HEAD_DIM)
        s_st[step, :, :HEAD_DIM] = jnp.sum(jnp.where(turn, peak, 0.0), axis=0, keepdims=True)
        s_st[step, :, HEAD_DIM:] = jnp.sum(jnp.where(turn, weight_sum, 0.0), axis=0, keepdims=True)
        slot = xx * NZ + zz
        for dz in FAR_Z:
            to = lax.rem(zz + dz, NZ)
            if (dx, dz) == (0, 0):
                pltpu.make_async_copy(o_st.at[step, to], obuf.at[slot], o_sem.at[1]).start()
                pltpu.make_async_copy(s_st.at[step], sbuf.at[slot], s_sem.at[1]).start()
            else:
                remote(s_st.at[step], sbuf.at[slot], s_sem.at[0], s_sem.at[1], at(dx, dz))
                remote(o_st.at[step, to], obuf.at[slot], o_sem.at[0], o_sem.at[1], at(dx, dz))

    wait(kbuf.at[core, xx], z_sem.at[1])
    wait(vbuf.at[core, xx], z_sem.at[3])
    remote(kbuf.at[core, xx], kbuf.at[core, xx], c_sem.at[0], c_sem.at[1], partner)
    remote(vbuf.at[core, xx], vbuf.at[core, xx], c_sem.at[2], c_sem.at[3], partner)
    for dx in (2, 1, 3):
        remote(kbuf.at[core, xx], kbuf.at[core, xx], x_sem.at[0], x_sem.at[1 + dx], at(dx, 0))
        remote(vbuf.at[core, xx], vbuf.at[core, xx], x_sem.at[1], x_sem.at[4 + dx], at(dx, 0))

    wait(kbuf.at[core, xx], c_sem.at[1])
    wait(vbuf.at[core, xx], c_sem.at[3])
    both = NC * NZ * ROWS
    col = iota((DRAFT, both), 1)
    col_token = ((col >> 4) & 7) * (NC * OWN) + (col >> 7) * OWN + (col & 3)
    expand = (iota((DRAFT, both), 0) == col_token).astype(F32).astype(BF16)
    allowed = dot(anc_rows.astype(BF16), expand) > 0.5
    wide_shape = (ROWS, both)
    allowed = allowed & (((iota(wide_shape, 1) >> 2) & 3) == ((iota(wide_shape, 0) >> 2) & 3))

    def request_rows(buf, r):
        return jnp.concatenate([buf[c, r].reshape(NZ * ROWS, HEAD_DIM) for c in range(NC)], axis=0)

    d_scores = jnp.where(allowed, nt_dot(q_own[...], request_rows(kbuf, xx)) * factor, NEG)
    d_peak = jnp.max(d_scores, axis=1, keepdims=True)
    d_weights = jnp.where(allowed, jnp.exp(d_scores - d_peak), 0.0)
    d_sum = jnp.sum(d_weights, axis=1, keepdims=True)
    d_out = dot(d_weights.astype(BF16), request_rows(vbuf, xx))

    for i, dx in enumerate((1, 3, 2)):
        r = lax.rem(xx + dx, NX)
        wait(kbuf.at[core, r], x_sem.at[1 + (NX - dx)])
        wait(vbuf.at[core, r], x_sem.at[4 + (NX - dx)])
        remote(kbuf.at[core, r], kbuf.at[core, r], c_sem.at[4 + 4 * i], c_sem.at[5 + 4 * i], partner)
        remote(vbuf.at[core, r], vbuf.at[core, r], c_sem.at[6 + 4 * i], c_sem.at[7 + 4 * i], partner)

    c_leaf.wait()
    p_place = (seq * BLOCK + iota((BLOCK, DRAFT), 0)).astype(F32)
    col_head = (iota((BLOCK, both), 1) >> 2) & 3
    for i, dx in enumerate((0, 1, 3, 2)):
        r = lax.rem(xx + dx, NX)
        if dx:
            wait(kbuf.at[core, r], c_sem.at[1 + 4 * i])
            wait(vbuf.at[core, r], c_sem.at[3 + 4 * i])
        anc = anc_s[r]
        target = jnp.sum(anc.astype(F32), axis=0, keepdims=True) - 1.0 + lens_s[r].astype(F32)
        leaf_hot = (iota((ROWS, DRAFT), 1) == leaf_s[r]).astype(F32).astype(BF16)
        on_path = nt_dot(leaf_hot, anc)[:1]
        placing = jnp.where((p_place == target) & (on_path > 0.5), 1.0, 0.0)
        written = jnp.sum(placing, axis=1, keepdims=True) > 0.5
        placing = dot(placing.astype(BF16), expand)
        k_rows = request_rows(kbuf, r)
        v_rows = request_rows(vbuf, r)
        for h in range(HEADS):
            columns = slice(h * HEAD_DIM, (h + 1) * HEAD_DIM)
            pick = jnp.where(col_head == h, placing, 0.0).astype(BF16)
            old_k = kfull[r, mine, columns].astype(F32)
            old_v = vfull[r, mine, columns].astype(F32)
            nk_s[r, :, columns] = jnp.where(written, dot(pick, k_rows), old_k).astype(BF16)
            nv_s[r, :, columns] = jnp.where(written, dot(pick, v_rows), old_v).astype(BF16)
    k_out = pltpu.make_async_copy(nk_s, out_k, out_sem.at[0])
    v_out = pltpu.make_async_copy(nv_s, out_v, out_sem.at[1])
    k_out.start()
    v_out.start()

    wait(sbuf, s_sem.at[1])
    wait(obuf, o_sem.at[1])
    peaks = sbuf[:, :, :HEAD_DIM]
    highest = jnp.max(peaks, axis=0)
    shares = jnp.exp(peaks - highest[None])
    sums = jnp.sum(shares * sbuf[:, :, HEAD_DIM:], axis=0)
    here = lane == zz * ROWS + iota(chunk, 0)

    def column(row):
        return jnp.sum(jnp.where(here, row, 0.0), axis=1, keepdims=True)

    top = column(highest)
    merged = None
    for s in range(NX * NZ):
        part = column(shares[s]) * obuf[s].astype(F32)
        merged = part if s == 0 else merged + part
    best = jnp.maximum(top, d_peak)
    c_share = jnp.exp(top - best)
    d_share = jnp.exp(d_peak - best)
    attention = (merged * c_share + d_out * d_share) / (column(sums) * c_share + d_sum * d_share)
    att_s[...] = attention
    att4 = jnp.concatenate([att_s[h * OWN : (h + 1) * OWN, :] for h in range(HEADS)], axis=1).astype(BF16)

    c_wo.wait()
    for n in range(NT):
        pr_s[n * OWN : (n + 1) * OWN, :] = dot(att4, wo_s[:, n * WIDTH : (n + 1) * WIDTH])
    pr_send[...] = pr_s[...].astype(BF16)
    for i, peer in enumerate(y_peers):
        remote(pr_send, pr_recv.at[i], p_sem.at[0], p_sem.at[1], peer)
    c_pg.wait()
    wait(pr_recv, p_sem.at[1])
    whole = pr_s[...] + pr_recv[0].astype(F32) + pr_recv[1].astype(F32) + pr_recv[2].astype(F32)
    pr_s[...] = whole
    quarters = [pr_s[n * OWN : (n + 1) * OWN, :] for n in range(NT)]
    squares = sum(part * part for part in quarters)
    power = jnp.sum(squares, axis=1, keepdims=True)
    own = quarters[0]
    for n in range(1, NT):
        own = jnp.where(tp == n, quarters[n], own)
    normed = own * lax.rsqrt(power / (NT * WIDTH) + EPS) * pg_s[...]
    residual = hid_s[:, pl.ds(pl.multiple_of(tp * WIDTH, WIDTH), WIDTH)].astype(F32)
    oh_s[...] = (residual + normed).astype(BF16)
    h_out = pltpu.make_async_copy(oh_s, out_h, out_sem.at[2])
    h_out.start()

    wait(sq_recv, sq_sem.at[0])
    wait(kfull.at[:, mine, :], swap_sem.at[0])
    wait(vfull.at[:, mine, :], swap_sem.at[2])
    wait(qbuf.at[pl.ds(0, NX * NZ - 1)], q_send)
    wait(kbuf.at[0, 0, pl.ds(0, NZ - 1)], z_sem.at[0])
    wait(vbuf.at[0, 0, pl.ds(0, NZ - 1)], z_sem.at[2])
    wait(kbuf.at[0, pl.ds(0, NX - 1)], x_sem.at[0])
    wait(vbuf.at[0, pl.ds(0, NX - 1)], x_sem.at[1])
    for i in range(NX):
        wait(kbuf.at[0, 0], c_sem.at[4 * i])
        wait(vbuf.at[0, 0], c_sem.at[4 * i + 2])
    wait(sbuf.at[pl.ds(0, NX * NZ - 1)], s_sem.at[0])
    wait(obuf.at[pl.ds(0, NX * NZ - 1)], o_sem.at[0])
    wait(pr_recv, p_sem.at[0])
    k_out.wait()
    v_out.wait()
    h_out.wait()


def body(hid, wq, wk, wv, wo, qg, kg, pg, kc, vc, lens, parents, leaf):
    half = np.arange(HEAD_DIM // 2, dtype=np.float32)
    freqs = np.power(np.float32(THETA), np.float32(-2.0) * half / np.float32(HEAD_DIM)).astype(np.float32)
    freq = jnp.asarray(np.concatenate([freqs, freqs])[None])
    vmem, sems = pltpu.VMEM, pltpu.SemaphoreType.DMA
    full = NC * BLOCK
    scratch = [
        vmem(hid.shape, BF16), vmem(wq.shape, BF16), vmem(wk.shape, BF16), vmem(wv.shape, BF16), vmem(wo.shape, BF16),
        vmem((1, WIDTH), F32), vmem((1, WIDTH), F32), vmem((1, WIDTH), F32),
        vmem(parents.shape, jnp.int32), vmem((1, HEAD_DIM), F32),
        pltpu.SMEM(lens.shape, jnp.int32), pltpu.SMEM(leaf.shape, jnp.int32),
        vmem((REQ, full, WIDTH), BF16), vmem((REQ, full, WIDTH), BF16), vmem((REQ, DRAFT, DRAFT), BF16),
        vmem((8, HEAD_DIM), F32), vmem((NT - 1, 8, HEAD_DIM), F32),
        vmem((ROWS, HEAD_DIM), BF16), vmem((ROWS, HEAD_DIM), BF16), vmem((ROWS, HEAD_DIM), BF16),
        vmem((NX * NZ, ROWS, HEAD_DIM), BF16),
        vmem((NC, NX, NZ, ROWS, HEAD_DIM), BF16), vmem((NC, NX, NZ, ROWS, HEAD_DIM), BF16),
        vmem((NX, NZ, ROWS, HEAD_DIM), BF16), vmem((NX, 1, 2 * HEAD_DIM), F32),
        vmem((NX * NZ, ROWS, HEAD_DIM), BF16), vmem((NX * NZ, 1, 2 * HEAD_DIM), F32),
        vmem((ROWS, HEAD_DIM), F32), vmem((ROWS, WIDTH), F32),
        vmem((ROWS, WIDTH), BF16), vmem((NT - 1, ROWS, WIDTH), BF16),
        vmem((REQ, BLOCK, WIDTH), BF16), vmem((REQ, BLOCK, WIDTH), BF16), vmem((OWN, WIDTH), BF16),
        sems((14,)), sems((4,)), sems((2,)), sems((NX,)), sems, sems((4,)), sems((8,)), sems((16,)),
        sems((2,)), sems((2,)), sems((2,)), sems((3,)),
    ]
    anywhere = pl.BlockSpec(memory_space=pltpu.HBM)
    return pl.pallas_call(
        kernel,
        out_shape=(
            jax.ShapeDtypeStruct((OWN, WIDTH), BF16),
            jax.ShapeDtypeStruct(kc.shape, BF16),
            jax.ShapeDtypeStruct(vc.shape, BF16),
        ),
        in_specs=[anywhere] * 14,
        out_specs=(anywhere,) * 3,
        scratch_shapes=scratch,
        compiler_params=pltpu.CompilerParams(
            collective_id=0, has_side_effects=True, vmem_limit_bytes=63 * 1024 * 1024
        ),
        cost_estimate=pl.CostEstimate(flops=300000000, bytes_accessed=11000000, transcendentals=200000),
        name="tree_attention",
    )(
        hid, wq, wk, wv, wo, qg.reshape(1, WIDTH), kg.reshape(1, WIDTH), pg.reshape(1, WIDTH),
        kc, vc, lens, parents, leaf, freq,
    )


def solution(mesh):
    return jax.shard_map(
        body,
        mesh=mesh,
        in_specs=(
            P("seq", None),
            P(None, "tp"),
            P(None, "tp"),
            P(None, "tp"),
            P("tp", None),
            P("tp"),
            P("tp"),
            P("tp"),
            P(None, "seq", "tp"),
            P(None, "seq", "tp"),
            P(),
            P(),
            P(),
        ),
        out_specs=(P("seq", "tp"), P(None, "seq", "tp"), P(None, "seq", "tp")),
        check_vma=False,
    )
```

time: 478 us -> 40.9 us (0.09); the launches traced: 471 us -> 40.7 us
  other arithmetic: 141 us -> 0 us
  waiting for transfers between devices: 115 us -> 0 us
  blocking collectives: 109 us -> 0 us
  local copies, waits for them, and re-layouts: 71 us -> 5.01 us
  Pallas kernels: 0 us -> 35 us
  matrix products: 17.9 us -> 0 us
  between operations: 14.6 us -> 0.64 us
    add x130 -> x0, other arithmetic: 132 us -> none  [the longest x63 87 us: join_partials(): out_first.reshape(rows_here, heads_here, -1) * scale_first[..., None]]
    all_gather x2 -> x0, waiting for transfers between devices: 114 us -> none  [the longest x1 79.4 us: body(): piece = lax.all_gather(hidden_in, 'seq', axis=0, tiled=True)]
    all_gather x2 -> x0, blocking collectives: 87.5 us -> none  [joined_2(): everything = jax.tree.map(lambda part: lax.all_gather(part, axis), x)]
    mul x126 -> x0, local copies, waits for them, and re-layouts: 42.2 us -> none  [the longest x63 21.1 us: join_partials(): out_first.reshape(rows_here, heads_here, -1) * scale_first[..., None]]
    pallas_call x0 -> x1, Pallas kernels: none -> 35 us  [body(): pl.pallas_call(kernel, out_shape=(jax.ShapeDtypeStruct((OWN, WIDTH), BF16...]
    psum x2 -> x0, blocking collectives: 21.7 us -> none  [the longest x1 13.1 us: body(): summed_heads = lax.psum(projected, 'tp')]
    dot_general x17 -> x0, matrix products: 17.9 us -> none  [the longest x1 2.62 us: body(): jnp.dot(piece, value_weight, preferred_element_type=jnp.float32)]
    exp x126 -> x0, local copies, waits for them, and re-layouts: 17.1 us -> none  [the longest x63 8.72 us: join_partials(): scale_first = jnp.exp(peak_first - highest)]
  transfers between devices with their start and end apart: 2 -> 0, of which waited for: 2 -> 0; matrix products, arithmetic and copies ran while one was open for 5% -> 0% of each run, Pallas kernels for 0% -> 0%
where the time goes in v1:
time: 40.9 us; the launch traced here: 40.7 us
  Pallas kernels  35 us (86%)
  local copies, waits for them, and re-layouts  5.01 us (12%)
  between operations  0.64 us (2%)
    pallas_call x1, Pallas kernels, body(): pl.pallas_call(kernel, out_shape=(jax.ShapeDtypeStruct((OWN, WIDTH), BF16...  35 us
    unnamed x3, local copies, waits for them, and re-layouts  5.01 us

profile of v1, /device:TPU:1, one launch (start us, length us, event | category | flops | bytes accessed | tf_op | source)
XLA Modules:
  0.0 40.7 jit_solution(14622744547495744486)
XLA Ops:
  0.6 35.0 %tree_attention.1 = (bf16[4,512]{1,0:T(4,128)(2,1)}, bf16[4,128,512]{2,1,0:T(8,128)(2,1)}, bf16[4,128,512]{2,1,0:T(8,128)(2,1)}) custom-call(bf16[4,2048]{1,0:T(4,128)(2,1)} %hid.1, bf16[2048,512]{1,0:T(8,128)(2,1)} %wq.1, bf16[2048,512]{1,0:T(8,128)(2,1)} %wk.1, bf16[2048,512]{1,0:T(8,128)(2,1)} %wv.1, bf16[512,2048]{1,0:T(8,128)(2,1)} %wo.1, ...), custom_call_target="tpu_custom_call" | custom-call | flops 300000000 | bytes 11000000 | tf_op jit(solution)/shard_map/tree_attention/pallas_call | solution.py:372
  35.7 1.3 %copy.20 = bf16[4,512]{1,0:T(4,128)(2,1)} copy(bf16[4,512]{1,0:T(4,128)(2,1)} %get-tuple-element.6) | data formatting | bytes 8192
  37.0 1.9 %copy.21 = bf16[4,128,512]{2,1,0:T(8,128)(2,1)} copy(bf16[4,128,512]{2,1,0:T(8,128)(2,1)} %get-tuple-element.7) | data formatting | bytes 1048576
  38.8 1.9 %copy.22 = bf16[4,128,512]{2,1,0:T(8,128)(2,1)} copy(bf16[4,128,512]{2,1,0:T(8,128)(2,1)} %get-tuple-element.8) | data formatting | bytes 1048576

commit v2 on v1

--- a/solution.py
+++ b/solution.py
@@ -23,6 +23,8 @@
 MESH = pl.DeviceIdType.MESH
 F32 = jnp.float32
 BF16 = jnp.bfloat16
+VMEM1 = 48 * 1024 * 1024
+VMEM2 = 16 * 1024 * 1024
 PLANES = (0, 1, 3, 2)
 FAR_Z = (4, 3, 5, 2, 6, 1, 7, 0)
 
@@ -50,8 +52,8 @@
     out_h, out_k, out_v,
     hid_s, wq_s, wk_s, wv_s, wo_s, qg_s, kg_s, pg_s, par_s, freq_s, lens_s, leaf_s,
     kfull, vfull, anc_s, sq_send, sq_recv, q_own, k_own, v_own, qbuf, kbuf, vbuf,
-    o_st, s_st, obuf, sbuf, att_s, pr_s, pr_send, pr_recv, nk_s, nv_s, oh_s,
-    lsem, swap_sem, sq_sem, q_sem, q_send, z_sem, x_sem, c_sem, o_sem, s_sem, p_sem, out_sem,
+    o_st, s_st, obuf, sbuf, att_s, pr_s, pr_send, pr_recv,
+    lsem, swap_sem, sq_sem, q_sem, q_send, z_sem, x_sem, c_sem, o_sem, s_sem, p_sem, plane_sem,
 ):
     seq = lax.axis_index("seq")
     tp = lax.axis_index("tp")
@@ -65,14 +67,16 @@
     partner = (seq + 1 - 2 * core, tp)
     y_peers = [(seq, lax.rem(tp + d, NT)) for d in range(1, NT)]
     plane_peers = [at(a, b) for a, b in far_first()]
+    x_peers = [at(a, 0) for a in range(1, NX)]
+    near_peers = [at(0, b) for b in range(1, NZ)] + x_peers + y_peers + [partner]
 
     barrier = pltpu.get_barrier_semaphore()
-    for peer in plane_peers + y_peers + [partner]:
+    for peer in near_peers:
         pl.semaphore_signal(barrier, inc=1, device_id=peer, device_id_type=MESH)
 
     pairs = [
-        (par, par_s), (lens, lens_s), (freq, freq_s), (hid, hid_s), (wq, wq_s), (wk, wk_s), (wv, wv_s),
-        (qg, qg_s), (kg, kg_s), (pg, pg_s), (leaf, leaf_s),
+        (par, par_s), (hid, hid_s), (wq, wq_s), (lens, lens_s), (freq, freq_s), (qg, qg_s), (kg, kg_s),
+        (wk, wk_s), (wv, wv_s), (pg, pg_s), (leaf, leaf_s),
         (kc, kfull.at[:, pl.ds(core * BLOCK, BLOCK), :]),
         (vc, vfull.at[:, pl.ds(core * BLOCK, BLOCK), :]),
         (wo, wo_s),
@@ -80,7 +84,7 @@
     local = [pltpu.make_async_copy(a, b, lsem.at[i]) for i, (a, b) in enumerate(pairs)]
     for copy in local:
         copy.start()
-    (c_par, c_lens, c_freq, c_hid, c_wq, c_wk, c_wv, c_qg, c_kg, c_pg, c_leaf, c_kc, c_vc, c_wo) = local
+    (c_par, c_hid, c_wq, c_lens, c_freq, c_qg, c_kg, c_wk, c_wv, c_pg, c_leaf, c_kc, c_vc, c_wo) = local
 
     def remote(src, dst, send, recv, peer):
         copy = pltpu.make_async_remote_copy(
@@ -132,44 +136,53 @@
     def spread(gain):
         return diagonal(jnp.broadcast_to(gain, (ROWS, WIDTH)))
 
+    lane8 = iota((8, HEAD_DIM), 1)
+
+    def turned(wide, gain):
+        x = diagonal(wide) * spread(gain)
+        return x * cosine + pltpu.roll(x, HEAD_DIM // 2, 1) * sine
+
+    def square_sum(wide):
+        return jnp.broadcast_to(jnp.sum(wide * wide, axis=1, keepdims=True)[:8], (8, HEAD_DIM))
+
+    def scaled(x, i):
+        wait(sq_recv.at[i], sq_sem.at[2 * i + 1])
+        total = sq_send[i] + sq_recv[i, 0] + sq_recv[i, 1] + sq_recv[i, 2]
+        scale = lax.rsqrt(total / (NT * WIDTH) + EPS)
+        return (x * jnp.concatenate([scale, scale], axis=0)).astype(BF16)
+
     c_wq.wait()
     q_wide = dot(h16, wq_s[...])
+    sq_send[0] = square_sum(q_wide)
+
+    pl.semaphore_wait(barrier, len(near_peers))
+    for i, peer in enumerate(y_peers):
+        remote(sq_send.at[0], sq_recv.at[0, i], sq_sem.at[0], sq_sem.at[1], peer)
+    for peer in x_peers:
+        pl.semaphore_signal(plane_sem, inc=1, device_id=peer, device_id_type=MESH)
+
+    for copy in (c_qg, c_kg):
+        copy.wait()
+    q_turn = turned(q_wide, qg_s[...])
     c_wk.wait()
     k_wide = dot(h16, wk_s[...])
-    q_sq = jnp.sum(q_wide * q_wide, axis=1, keepdims=True)
-    k_sq = jnp.sum(k_wide * k_wide, axis=1, keepdims=True)
-    lane8 = iota((8, HEAD_DIM), 1)
-    sq_mine = jnp.where(lane8 < HEAD_DIM // 2, q_sq[:8], k_sq[:8])
-    sq_send[...] = sq_mine
-    c_wv.wait()
-    v_own[...] = diagonal(dot(h16, wv_s[...])).astype(BF16)
-    for copy in (c_qg, c_kg):
-        copy.wait()
-    q_turn = diagonal(q_wide) * spread(qg_s[...])
-    k_turn = diagonal(k_wide) * spread(kg_s[...])
-    q_turn = q_turn * cosine + pltpu.roll(q_turn, HEAD_DIM // 2, 1) * sine
-    k_turn = k_turn * cosine + pltpu.roll(k_turn, HEAD_DIM // 2, 1) * sine
-
-    pl.semaphore_wait(barrier, len(plane_peers) + len(y_peers) + 1)
-
+    sq_send[1] = square_sum(k_wide)
     for i, peer in enumerate(y_peers):
-        remote(sq_send, sq_recv.at[i], sq_sem.at[0], sq_sem.at[1], peer)
+        remote(sq_send.at[1], sq_recv.at[1, i], sq_sem.at[2], sq_sem.at[3], peer)
     mine = pl.ds(core * BLOCK, BLOCK)
     remote(kc, kfull.at[:, mine, :], swap_sem.at[0], swap_sem.at[1], partner)
     remote(vc, vfull.at[:, mine, :], swap_sem.at[2], swap_sem.at[3], partner)
-
-    wait(sq_recv, sq_sem.at[1])
-    total = sq_mine + sq_recv[0] + sq_recv[1] + sq_recv[2]
-    scale = lax.rsqrt(total / (NT * WIDTH) + EPS)
-    other = pltpu.roll(scale, HEAD_DIM // 2, 1)
-    q_scale = jnp.where(lane8 < HEAD_DIM // 2, scale, other)
-    k_scale = jnp.where(lane8 < HEAD_DIM // 2, other, scale)
-    q_own[...] = (q_turn * jnp.concatenate([q_scale, q_scale], axis=0)).astype(BF16)
-    k_own[...] = (k_turn * jnp.concatenate([k_scale, k_scale], axis=0)).astype(BF16)
+    k_turn = turned(k_wide, kg_s[...])
+    c_wv.wait()
+    v_own[...] = diagonal(dot(h16, wv_s[...])).astype(BF16)
+
+    q_own[...] = scaled(q_turn, 0)
+    pl.semaphore_wait(plane_sem, len(x_peers))
 
     for peer in plane_peers:
         remote(q_own, qbuf.at[xx * NZ + zz], q_send, q_sem.at[xx], peer)
     pltpu.make_async_copy(q_own, qbuf.at[xx * NZ + zz], q_sem.at[xx]).start()
+    k_own[...] = scaled(k_turn, 1)
     for dz in FAR_Z[:-1]:
         remote(k_own, kbuf.at[core, xx, zz], z_sem.at[0], z_sem.at[1], at(0, dz))
         remote(v_own, vbuf.at[core, xx, zz], z_sem.at[2], z_sem.at[3], at(0, dz))
@@ -254,7 +267,8 @@
     c_leaf.wait()
     p_place = (seq * BLOCK + iota((BLOCK, DRAFT), 0)).astype(F32)
     col_head = (iota((BLOCK, both), 1) >> 2) & 3
-    for i, dx in enumerate((0, 1, 3, 2)):
+
+    def compact(i, dx):
         r = lax.rem(xx + dx, NX)
         if dx:
             wait(kbuf.at[core, r], c_sem.at[1 + 4 * i])
@@ -273,12 +287,10 @@
             pick = jnp.where(col_head == h, placing, 0.0).astype(BF16)
             old_k = kfull[r, mine, columns].astype(F32)
             old_v = vfull[r, mine, columns].astype(F32)
-            nk_s[r, :, columns] = jnp.where(written, dot(pick, k_rows), old_k).astype(BF16)
-            nv_s[r, :, columns] = jnp.where(written, dot(pick, v_rows), old_v).astype(BF16)
-    k_out = pltpu.make_async_copy(nk_s, out_k, out_sem.at[0])
-    v_out = pltpu.make_async_copy(nv_s, out_v, out_sem.at[1])
-    k_out.start()
-    v_out.start()
+            out_k[r, :, columns] = jnp.where(written, dot(pick, k_rows), old_k).astype(BF16)
+            out_v[r, :, columns] = jnp.where(written, dot(pick, v_rows), old_v).astype(BF16)
+
+    compact(0, 0)
 
     wait(sbuf, s_sem.at[1])
     wait(obuf, o_sem.at[1])
@@ -309,6 +321,8 @@
     pr_send[...] = pr_s[...].astype(BF16)
     for i, peer in enumerate(y_peers):
         remote(pr_send, pr_recv.at[i], p_sem.at[0], p_sem.at[1], peer)
+    for i, dx in enumerate((1, 3, 2)):
+        compact(i + 1, dx)
     c_pg.wait()
     wait(pr_recv, p_sem.at[1])
     whole = pr_s[...] + pr_recv[0].astype(F32) + pr_recv[1].astype(F32) + pr_recv[2].astype(F32)
@@ -321,11 +335,10 @@
         own = jnp.where(tp == n, quarters[n], own)
     normed = own * lax.rsqrt(power / (NT * WIDTH) + EPS) * pg_s[...]
     residual = hid_s[:, pl.ds(pl.multiple_of(tp * WIDTH, WIDTH), WIDTH)].astype(F32)
-    oh_s[...] = (residual + normed).astype(BF16)
-    h_out = pltpu.make_async_copy(oh_s, out_h, out_sem.at[2])
-    h_out.start()
-
-    wait(sq_recv, sq_sem.at[0])
+    out_h[...] = (residual + normed).astype(BF16)
+
+    wait(sq_recv.at[0], sq_sem.at[0])
+    wait(sq_recv.at[1], sq_sem.at[2])
     wait(kfull.at[:, mine, :], swap_sem.at[0])
     wait(vfull.at[:, mine, :], swap_sem.at[2])
     wait(qbuf.at[pl.ds(0, NX * NZ - 1)], q_send)
@@ -339,9 +352,17 @@
     wait(sbuf.at[pl.ds(0, NX * NZ - 1)], s_sem.at[0])
     wait(obuf.at[pl.ds(0, NX * NZ - 1)], o_sem.at[0])
     wait(pr_recv, p_sem.at[0])
-    k_out.wait()
-    v_out.wait()
-    h_out.wait()
+
+
+def hand_out(a, b, c, out_a, out_b, out_c, sem):
+    copies = [
+        pltpu.make_async_copy(src, dst, sem.at[i])
+        for i, (src, dst) in enumerate(((b, out_b), (c, out_c), (a, out_a)))
+    ]
+    for copy in copies:
+        copy.start()
+    for copy in copies:
+        copy.wait()
 
 
 def body(hid, wq, wk, wv, wo, qg, kg, pg, kc, vc, lens, parents, leaf):
@@ -356,7 +377,7 @@
         vmem(parents.shape, jnp.int32), vmem((1, HEAD_DIM), F32),
         pltpu.SMEM(lens.shape, jnp.int32), pltpu.SMEM(leaf.shape, jnp.int32),
         vmem((REQ, full, WIDTH), BF16), vmem((REQ, full, WIDTH), BF16), vmem((REQ, DRAFT, DRAFT), BF16),
-        vmem((8, HEAD_DIM), F32), vmem((NT - 1, 8, HEAD_DIM), F32),
+        vmem((2, 8, HEAD_DIM), F32), vmem((2, NT - 1, 8, HEAD_DIM), F32),
         vmem((ROWS, HEAD_DIM), BF16), vmem((ROWS, HEAD_DIM), BF16), vmem((ROWS, HEAD_DIM), BF16),
         vmem((NX * NZ, ROWS, HEAD_DIM), BF16),
         vmem((NC, NX, NZ, ROWS, HEAD_DIM), BF16), vmem((NC, NX, NZ, ROWS, HEAD_DIM), BF16),
@@ -364,30 +385,35 @@
         vmem((NX * NZ, ROWS, HEAD_DIM), BF16), vmem((NX * NZ, 1, 2 * HEAD_DIM), F32),
         vmem((ROWS, HEAD_DIM), F32), vmem((ROWS, WIDTH), F32),
         vmem((ROWS, WIDTH), BF16), vmem((NT - 1, ROWS, WIDTH), BF16),
-        vmem((REQ, BLOCK, WIDTH), BF16), vmem((REQ, BLOCK, WIDTH), BF16), vmem((OWN, WIDTH), BF16),
-        sems((14,)), sems((4,)), sems((2,)), sems((NX,)), sems, sems((4,)), sems((8,)), sems((16,)),
-        sems((2,)), sems((2,)), sems((2,)), sems((3,)),
+        sems((14,)), sems((4,)), sems((4,)), sems((NX,)), sems, sems((4,)), sems((8,)), sems((16,)),
+        sems((2,)), sems((2,)), sems((2,)), pltpu.SemaphoreType.REGULAR,
     ]
     anywhere = pl.BlockSpec(memory_space=pltpu.HBM)
-    return pl.pallas_call(
+    results = pl.pallas_call(
         kernel,
-        out_shape=(
-            jax.ShapeDtypeStruct((OWN, WIDTH), BF16),
-            jax.ShapeDtypeStruct(kc.shape, BF16),
-            jax.ShapeDtypeStruct(vc.shape, BF16),
-        ),
+        out_shape=(vmem((OWN, WIDTH), BF16), vmem(kc.shape, BF16), vmem(vc.shape, BF16)),
         in_specs=[anywhere] * 14,
-        out_specs=(anywhere,) * 3,
+        out_specs=(pl.BlockSpec(memory_space=pltpu.VMEM),) * 3,
         scratch_shapes=scratch,
         compiler_params=pltpu.CompilerParams(
-            collective_id=0, has_side_effects=True, vmem_limit_bytes=63 * 1024 * 1024
+            collective_id=0, has_side_effects=True, vmem_limit_bytes=VMEM1
         ),
         cost_estimate=pl.CostEstimate(flops=300000000, bytes_accessed=11000000, transcendentals=200000),
         name="tree_attention",
-    )(
+    )(*(pltpu.with_memory_space_constraint(part, pltpu.HBM) for part in (
         hid, wq, wk, wv, wo, qg.reshape(1, WIDTH), kg.reshape(1, WIDTH), pg.reshape(1, WIDTH),
         kc, vc, lens, parents, leaf, freq,
-    )
+    )))
+    return pl.pallas_call(
+        hand_out,
+        out_shape=tuple(jax.ShapeDtypeStruct(part.shape, part.dtype) for part in results),
+        in_specs=[pl.BlockSpec(memory_space=pltpu.VMEM)] * 3,
+        out_specs=(anywhere,) * 3,
+        scratch_shapes=[sems((3,))],
+        compiler_params=pltpu.CompilerParams(vmem_limit_bytes=VMEM2),
+        cost_estimate=pl.CostEstimate(flops=0, bytes_accessed=2200000, transcendentals=0),
+        name="hand_out",
+    )(*results)
 
 
 def solution(mesh):

time: 40.9 us -> 32.1 us (0.78)
  the two profiles are of different devices: /device:TPU:1 before, /device:TPU:32 now
where the time goes in v2:
time: 32.1 us; the launch traced here: 32 us
  Pallas kernels  31.4 us (98%)
  between operations  0.64 us (2%)
    pallas_call x1, Pallas kernels, body(): pl.pallas_call(kernel, out_shape=(vmem((OWN, WIDTH), BF16), vmem(kc.shape...  30.4 us
    pallas_call x1, Pallas kernels, body(): pl.pallas_call(hand_out, out_shape=tuple((jax.ShapeDtypeStruct(part.shape...  1 us

profile of v2, /device:TPU:32, one launch (start us, length us, event | category | flops | bytes accessed | tf_op | source)
XLA Modules:
  0.0 32.0 jit_solution(11319165850477132124)
XLA Ops:
  0.6 30.4 %tree_attention.1 = (bf16[4,512]{1,0:T(4,128)(2,1)S(1)}, bf16[4,128,512]{2,1,0:T(8,128)(2,1)S(1)}, bf16[4,128,512]{2,1,0:T(8,128)(2,1)S(1)}) custom-call(bf16[4,2048]{1,0:T(4,128)(2,1)} %hid.1, bf16[2048,512]{1,0:T(8,128)(2,1)} %wq.1, bf16[2048,512]{1,0:T(8,128)(2,1)} %wk.1, bf16[2048,512]{1,0:T(8,128)(2,1)} %wv.1, bf16[512,2048]{1,0:T(8,128)(2,1)} %wo.1, ...), custom_call_target="tpu_custom_call" | custom-call | flops 300000000 | bytes 11000000 | tf_op jit(solution)/shard_map/tree_attention/pallas_call | solution.py:392
  31.0 1.0 %hand_out.1 = (bf16[4,512]{1,0:T(4,128)(2,1)}, bf16[4,128,512]{2,1,0:T(8,128)(2,1)}, bf16[4,128,512]{2,1,0:T(8,128)(2,1)}) custom-call(bf16[4,512]{1,0:T(4,128)(2,1)S(1)} %get-tuple-element.6.a, bf16[4,128,512]{2,1,0:T(8,128)(2,1)S(1)} %get-tuple-element.7.b, bf16[4,128,512]{2,1,0:T(8,128)(2,1)S(1)} %get-tuple-element.8.c), custom_call_target="tpu_custom_call" | custom-call | bytes 2200000 | tf_op jit(solution)/shard_map/hand_out/pallas_call | solution.py:407

commit v3 on v2

--- a/solution.py
+++ b/solution.py
@@ -25,7 +25,7 @@
 BF16 = jnp.bfloat16
 VMEM1 = 48 * 1024 * 1024
 VMEM2 = 16 * 1024 * 1024
-PLANES = (0, 1, 3, 2)
+PLANES = (2, 1, 3, 0)
 FAR_Z = (4, 3, 5, 2, 6, 1, 7, 0)
 
 
@@ -175,6 +175,9 @@
     k_turn = turned(k_wide, kg_s[...])
     c_wv.wait()
     v_own[...] = diagonal(dot(h16, wv_s[...])).astype(BF16)
+    for dz in FAR_Z[:-1]:
+        remote(v_own, vbuf.at[core, xx, zz], z_sem.at[2], z_sem.at[3], at(0, dz))
+    pltpu.make_async_copy(v_own, vbuf.at[core, xx, zz], z_sem.at[3]).start()
 
     q_own[...] = scaled(q_turn, 0)
     pl.semaphore_wait(plane_sem, len(x_peers))
@@ -185,9 +188,13 @@
     k_own[...] = scaled(k_turn, 1)
     for dz in FAR_Z[:-1]:
         remote(k_own, kbuf.at[core, xx, zz], z_sem.at[0], z_sem.at[1], at(0, dz))
-        remote(v_own, vbuf.at[core, xx, zz], z_sem.at[2], z_sem.at[3], at(0, dz))
     pltpu.make_async_copy(k_own, kbuf.at[core, xx, zz], z_sem.at[1]).start()
-    pltpu.make_async_copy(v_own, vbuf.at[core, xx, zz], z_sem.at[3]).start()
+
+    def onward(buf, sem, first, at_x, at_c):
+        wait(buf.at[core, xx], z_sem.at[sem])
+        for far in (2, 1, 3):
+            remote(buf.at[core, xx], buf.at[core, xx], x_sem.at[first], x_sem.at[at_x + far], at(far, 0))
+        remote(buf.at[core, xx], buf.at[core, xx], c_sem.at[at_c], c_sem.at[at_c + 1], partner)
 
     factor = 1.0 / math.sqrt(HEAD_DIM)
     tall = (NZ * ROWS, NC * BLOCK)
@@ -199,6 +206,10 @@
     wait(kfull.at[:, mine, :], swap_sem.at[1])
     wait(vfull.at[:, mine, :], swap_sem.at[3])
     for step, dx in enumerate(PLANES):
+        if step == 0:
+            onward(vbuf, 3, 1, 4, 2)
+        if step == 3:
+            onward(kbuf, 1, 0, 1, 0)
         r = lax.rem(xx + dx, NX)
         group = pl.ds(r * NZ, NZ)
         wait(qbuf.at[group], q_sem.at[r])
@@ -229,14 +240,6 @@
             else:
                 remote(s_st.at[step], sbuf.at[slot], s_sem.at[0], s_sem.at[1], at(dx, dz))
                 remote(o_st.at[step, to], obuf.at[slot], o_sem.at[0], o_sem.at[1], at(dx, dz))
-
-    wait(kbuf.at[core, xx], z_sem.at[1])
-    wait(vbuf.at[core, xx], z_sem.at[3])
-    remote(kbuf.at[core, xx], kbuf.at[core, xx], c_sem.at[0], c_sem.at[1], partner)
-    remote(vbuf.at[core, xx], vbuf.at[core, xx], c_sem.at[2], c_sem.at[3], partner)
-    for dx in (2, 1, 3):
-        remote(kbuf.at[core, xx], kbuf.at[core, xx], x_sem.at[0], x_sem.at[1 + dx], at(dx, 0))
-        remote(vbuf.at[core, xx], vbuf.at[core, xx], x_sem.at[1], x_sem.at[4 + dx], at(dx, 0))
 
     wait(kbuf.at[core, xx], c_sem.at[1])
     wait(vbuf.at[core, xx], c_sem.at[3])

time: 32.1 us -> 31.7 us (0.988)
  the two profiles are of different devices: /device:TPU:32 before, /device:TPU:6 now
where the time goes in v3:
time: 31.7 us; the launch traced here: 31.6 us
  Pallas kernels  30.9 us (97%)
  between operations  0.64 us (2%)
    pallas_call x1, Pallas kernels, body(): pl.pallas_call(kernel, out_shape=(vmem((OWN, WIDTH), BF16), vmem(kc.shape...  30 us
    pallas_call x1, Pallas kernels, body(): pl.pallas_call(hand_out, out_shape=tuple((jax.ShapeDtypeStruct(part.shape...  1 us

profile of v3, /device:TPU:6, one launch (start us, length us, event | category | flops | bytes accessed | tf_op | source)
XLA Modules:
  0.0 31.6 jit_solution(14084571335112544916)
XLA Ops:
  0.6 30.0 %tree_attention.1 = (bf16[4,512]{1,0:T(4,128)(2,1)S(1)}, bf16[4,128,512]{2,1,0:T(8,128)(2,1)S(1)}, bf16[4,128,512]{2,1,0:T(8,128)(2,1)S(1)}) custom-call(bf16[4,2048]{1,0:T(4,128)(2,1)} %hid.1, bf16[2048,512]{1,0:T(8,128)(2,1)} %wq.1, bf16[2048,512]{1,0:T(8,128)(2,1)} %wk.1, bf16[2048,512]{1,0:T(8,128)(2,1)} %wv.1, bf16[512,2048]{1,0:T(8,128)(2,1)} %wo.1, ...), custom_call_target="tpu_custom_call" | custom-call | flops 300000000 | bytes 11000000 | tf_op jit(solution)/shard_map/tree_attention/pallas_call | solution.py:395
  30.6 1.0 %hand_out.1 = (bf16[4,512]{1,0:T(4,128)(2,1)}, bf16[4,128,512]{2,1,0:T(8,128)(2,1)}, bf16[4,128,512]{2,1,0:T(8,128)(2,1)}) custom-call(bf16[4,512]{1,0:T(4,128)(2,1)S(1)} %get-tuple-element.6.a, bf16[4,128,512]{2,1,0:T(8,128)(2,1)S(1)} %get-tuple-element.7.b, bf16[4,128,512]{2,1,0:T(8,128)(2,1)S(1)} %get-tuple-element.8.c), custom_call_target="tpu_custom_call" | custom-call | bytes 2200000 | tf_op jit(solution)/shard_map/hand_out/pallas_call | solution.py:410

commit v4 on v3

--- a/solution.py
+++ b/solution.py
@@ -61,18 +61,23 @@
     zz = lax.rem(seq // NC, NZ)
     xx = seq // (NC * NZ)
 
-    def at(dx, dz):
-        return ((lax.rem(xx + dx, NX) * NZ + lax.rem(zz + dz, NZ)) * NC + core, tp)
+    def at(dx, dz, on=core):
+        return ((lax.rem(xx + dx, NX) * NZ + lax.rem(zz + dz, NZ)) * NC + on, tp)
 
     partner = (seq + 1 - 2 * core, tp)
     y_peers = [(seq, lax.rem(tp + d, NT)) for d in range(1, NT)]
-    plane_peers = [at(a, b) for a, b in far_first()]
+    plane_peers = [at(a, b, 1) for a, b in far_first()]
     x_peers = [at(a, 0) for a in range(1, NX)]
     near_peers = [at(0, b) for b in range(1, NZ)] + x_peers + y_peers + [partner]
 
     barrier = pltpu.get_barrier_semaphore()
     for peer in near_peers:
         pl.semaphore_signal(barrier, inc=1, device_id=peer, device_id_type=MESH)
+
+    @pl.when(core == 1)
+    def _():
+        for dz in range(1, NZ):
+            pl.semaphore_signal(barrier, inc=1, device_id=at(0, dz, 0), device_id_type=MESH)
 
     pairs = [
         (par, par_s), (hid, hid_s), (wq, wq_s), (lens, lens_s), (freq, freq_s), (qg, qg_s), (kg, kg_s),
@@ -110,9 +115,13 @@
     chunk = (ROWS, HEAD_DIM)
     row_head = (iota(chunk, 0) >> 2) & 3
     lane = iota(chunk, 1)
-    row_token = (zz * NC + core) * OWN + (iota((ROWS, DRAFT), 0) & 3)
-    one_hot = (iota((ROWS, DRAFT), 1) == row_token).astype(F32).astype(BF16)
-    anc_rows = nt_dot(one_hot, anc_s[xx])
+
+    def ancestors_of(c):
+        row_token = (zz * NC + c) * OWN + (iota((ROWS, DRAFT), 0) & 3)
+        one_hot = (iota((ROWS, DRAFT), 1) == row_token).astype(F32).astype(BF16)
+        return nt_dot(one_hot, anc_s[xx])
+
+    anc_rows = ancestors_of(core)
     depth = jnp.sum(anc_rows, axis=1, keepdims=True) - 1.0
     c_lens.wait()
     position = lens_s[xx].astype(F32) + depth
@@ -155,7 +164,7 @@
     q_wide = dot(h16, wq_s[...])
     sq_send[0] = square_sum(q_wide)
 
-    pl.semaphore_wait(barrier, len(near_peers))
+    pl.semaphore_wait(barrier, len(near_peers) + (NZ - 1) * (1 - core))
     for i, peer in enumerate(y_peers):
         remote(sq_send.at[0], sq_recv.at[0, i], sq_sem.at[0], sq_sem.at[1], peer)
     for peer in x_peers:
@@ -170,8 +179,13 @@
     for i, peer in enumerate(y_peers):
         remote(sq_send.at[1], sq_recv.at[1, i], sq_sem.at[2], sq_sem.at[3], peer)
     mine = pl.ds(core * BLOCK, BLOCK)
-    remote(kc, kfull.at[:, mine, :], swap_sem.at[0], swap_sem.at[1], partner)
-    remote(vc, vfull.at[:, mine, :], swap_sem.at[2], swap_sem.at[3], partner)
+    first_block = pl.ds(0, BLOCK)
+
+    @pl.when(core == 0)
+    def _():
+        remote(kc, kfull.at[:, first_block, :], swap_sem.at[0], swap_sem.at[1], partner)
+        remote(vc, vfull.at[:, first_block, :], swap_sem.at[2], swap_sem.at[3], partner)
+
     k_turn = turned(k_wide, kg_s[...])
     c_wv.wait()
     v_own[...] = diagonal(dot(h16, wv_s[...])).astype(BF16)
@@ -182,9 +196,19 @@
     q_own[...] = scaled(q_turn, 0)
     pl.semaphore_wait(plane_sem, len(x_peers))
 
+    slot = xx * NZ + zz
+    q_ready = q_sem.at[core * NX + xx]
     for peer in plane_peers:
-        remote(q_own, qbuf.at[xx * NZ + zz], q_send, q_sem.at[xx], peer)
-    pltpu.make_async_copy(q_own, qbuf.at[xx * NZ + zz], q_sem.at[xx]).start()
+        remote(q_own, qbuf.at[core * NX * NZ + slot], q_send, q_ready, peer)
+
+    @pl.when(core == 0)
+    def _():
+        remote(q_own, qbuf.at[slot], q_send, q_ready, partner)
+
+    @pl.when(core == 1)
+    def _():
+        pltpu.make_async_copy(q_own, qbuf.at[NX * NZ + slot], q_ready).start()
+
     k_own[...] = scaled(k_turn, 1)
     for dz in FAR_Z[:-1]:
         remote(k_own, kbuf.at[core, xx, zz], z_sem.at[0], z_sem.at[1], at(0, dz))
@@ -197,49 +221,56 @@
         remote(buf.at[core, xx], buf.at[core, xx], c_sem.at[at_c], c_sem.at[at_c + 1], partner)
 
     factor = 1.0 / math.sqrt(HEAD_DIM)
-    tall = (NZ * ROWS, NC * BLOCK)
-    tall_head = (iota(tall, 0) >> 2) & 3
-    place = (seq - core) * BLOCK + iota(tall, 1)
-    turn = iota((NZ * ROWS, HEAD_DIM), 0) == iota((NZ * ROWS, HEAD_DIM), 1)
     c_kc.wait()
     c_vc.wait()
-    wait(kfull.at[:, mine, :], swap_sem.at[1])
-    wait(vfull.at[:, mine, :], swap_sem.at[3])
-    for step, dx in enumerate(PLANES):
-        if step == 0:
-            onward(vbuf, 3, 1, 4, 2)
-        if step == 3:
-            onward(kbuf, 1, 0, 1, 0)
-        r = lax.rem(xx + dx, NX)
-        group = pl.ds(r * NZ, NZ)
-        wait(qbuf.at[group], q_sem.at[r])
-        queries = qbuf[group].reshape(NZ * ROWS, HEAD_DIM)
-        scores = None
-        for h in range(HEADS):
-            part = nt_dot(queries, kfull[r, :, h * HEAD_DIM : (h + 1) * HEAD_DIM])
-            scores = part if h == 0 else jnp.where(tall_head == h, part, scores)
-        visible = place < lens_s[r]
-        scores = jnp.where(visible, scores * factor, NEG)
-        peak = jnp.max(scores, axis=1, keepdims=True)
-        weights = jnp.where(visible, jnp.exp(scores - peak), 0.0)
-        weight_sum = jnp.sum(weights, axis=1, keepdims=True)
-        mixed = None
-        for h in range(HEADS):
-            masked = jnp.where(tall_head == h, weights, 0.0).astype(BF16)
-            part = dot(masked, vfull[r, :, h * HEAD_DIM : (h + 1) * HEAD_DIM])
-            mixed = part if h == 0 else mixed + part
-        o_st[step] = mixed.astype(BF16).reshape(NZ, ROWS, HEAD_DIM)
-        s_st[step, :, :HEAD_DIM] = jnp.sum(jnp.where(turn, peak, 0.0), axis=0, keepdims=True)
-        s_st[step, :, HEAD_DIM:] = jnp.sum(jnp.where(turn, weight_sum, 0.0), axis=0, keepdims=True)
-        slot = xx * NZ + zz
-        for dz in FAR_Z:
-            to = lax.rem(zz + dz, NZ)
-            if (dx, dz) == (0, 0):
-                pltpu.make_async_copy(o_st.at[step, to], obuf.at[slot], o_sem.at[1]).start()
-                pltpu.make_async_copy(s_st.at[step], sbuf.at[slot], s_sem.at[1]).start()
-            else:
-                remote(s_st.at[step], sbuf.at[slot], s_sem.at[0], s_sem.at[1], at(dx, dz))
-                remote(o_st.at[step, to], obuf.at[slot], o_sem.at[0], o_sem.at[1], at(dx, dz))
+
+    @pl.when(core == 0)
+    def _():
+        onward(vbuf, 3, 1, 4, 2)
+        onward(kbuf, 1, 0, 1, 0)
+
+    @pl.when(core == 1)
+    def _():
+        tall = (NZ * ROWS, NC * BLOCK)
+        tall_head = (iota(tall, 0) >> 2) & 3
+        place = (seq - 1) * BLOCK + iota(tall, 1)
+        turn = iota((NZ * ROWS, HEAD_DIM), 0) == iota((NZ * ROWS, HEAD_DIM), 1)
+        onward(vbuf, 3, 1, 4, 2)
+        wait(kfull.at[:, first_block, :], swap_sem.at[1])
+        wait(vfull.at[:, first_block, :], swap_sem.at[3])
+        for step, (c, dx) in enumerate([(c, dx) for c in (1, 0) for dx in PLANES]):
+            if step == 2:
+                onward(kbuf, 1, 0, 1, 0)
+            r = lax.rem(xx + dx, NX)
+            group = pl.ds((c * NX + r) * NZ, NZ)
+            wait(qbuf.at[group], q_sem.at[c * NX + r])
+            queries = qbuf[group].reshape(NZ * ROWS, HEAD_DIM)
+            scores = None
+            for h in range(HEADS):
+                part = nt_dot(queries, kfull[r, :, h * HEAD_DIM : (h + 1) * HEAD_DIM])
+                scores = part if h == 0 else jnp.where(tall_head == h, part, scores)
+            visible = place < lens_s[r]
+            scores = jnp.where(visible, scores * factor, NEG)
+            peak = jnp.max(scores, axis=1, keepdims=True)
+            weights = jnp.where(visible, jnp.exp(scores - peak), 0.0)
+            weight_sum = jnp.sum(weights, axis=1, keepdims=True)
+            mixed = None
+            for h in range(HEADS):
+                masked = jnp.where(tall_head == h, weights, 0.0).astype(BF16)
+                part = dot(masked, vfull[r, :, h * HEAD_DIM : (h + 1) * HEAD_DIM])
+                mixed = part if h == 0 else mixed + part
+            o_st[step] = mixed.astype(BF16).reshape(NZ, ROWS, HEAD_DIM)
+            s_st[step, :, :HEAD_DIM] = jnp.sum(jnp.where(turn, peak, 0.0), axis=0, keepdims=True)
+            s_st[step, :, HEAD_DIM:] = jnp.sum(jnp.where(turn, weight_sum, 0.0), axis=0, keepdims=True)
+            there = c * NX * NZ + slot
+            for dz in FAR_Z:
+                to = lax.rem(zz + dz, NZ)
+                if (dx, dz) == (0, 0):
+                    pltpu.make_async_copy(o_st.at[step, to], obuf.at[there], o_sem.at[1 + c]).start()
+                    pltpu.make_async_copy(s_st.at[step], sbuf.at[there], s_sem.at[1 + c]).start()
+                else:
+                    remote(s_st.at[step], sbuf.at[there], s_sem.at[0], s_sem.at[1 + c], at(dx, dz))
+                    remote(o_st.at[step, to], obuf.at[there], o_sem.at[0], o_sem.at[1 + c], at(dx, dz))
 
     wait(kbuf.at[core, xx], c_sem.at[1])
     wait(vbuf.at[core, xx], c_sem.at[3])
@@ -247,18 +278,9 @@
     col = iota((DRAFT, both), 1)
     col_token = ((col >> 4) & 7) * (NC * OWN) + (col >> 7) * OWN + (col & 3)
     expand = (iota((DRAFT, both), 0) == col_token).astype(F32).astype(BF16)
-    allowed = dot(anc_rows.astype(BF16), expand) > 0.5
-    wide_shape = (ROWS, both)
-    allowed = allowed & (((iota(wide_shape, 1) >> 2) & 3) == ((iota(wide_shape, 0) >> 2) & 3))
 
     def request_rows(buf, r):
         return jnp.concatenate([buf[c, r].reshape(NZ * ROWS, HEAD_DIM) for c in range(NC)], axis=0)
-
-    d_scores = jnp.where(allowed, nt_dot(q_own[...], request_rows(kbuf, xx)) * factor, NEG)
-    d_peak = jnp.max(d_scores, axis=1, keepdims=True)
-    d_weights = jnp.where(allowed, jnp.exp(d_scores - d_peak), 0.0)
-    d_sum = jnp.sum(d_weights, axis=1, keepdims=True)
-    d_out = dot(d_weights.astype(BF16), request_rows(vbuf, xx))
 
     for i, dx in enumerate((1, 3, 2)):
         r = lax.rem(xx + dx, NX)
@@ -295,40 +317,73 @@
 
     compact(0, 0)
 
-    wait(sbuf, s_sem.at[1])
-    wait(obuf, o_sem.at[1])
-    peaks = sbuf[:, :, :HEAD_DIM]
-    highest = jnp.max(peaks, axis=0)
-    shares = jnp.exp(peaks - highest[None])
-    sums = jnp.sum(shares * sbuf[:, :, HEAD_DIM:], axis=0)
-    here = lane == zz * ROWS + iota(chunk, 0)
-
-    def column(row):
-        return jnp.sum(jnp.where(here, row, 0.0), axis=1, keepdims=True)
-
-    top = column(highest)
-    merged = None
-    for s in range(NX * NZ):
-        part = column(shares[s]) * obuf[s].astype(F32)
-        merged = part if s == 0 else merged + part
-    best = jnp.maximum(top, d_peak)
-    c_share = jnp.exp(top - best)
-    d_share = jnp.exp(d_peak - best)
-    attention = (merged * c_share + d_out * d_share) / (column(sums) * c_share + d_sum * d_share)
-    att_s[...] = attention
-    att4 = jnp.concatenate([att_s[h * OWN : (h + 1) * OWN, :] for h in range(HEADS)], axis=1).astype(BF16)
-
-    c_wo.wait()
-    for n in range(NT):
-        pr_s[n * OWN : (n + 1) * OWN, :] = dot(att4, wo_s[:, n * WIDTH : (n + 1) * WIDTH])
-    pr_send[...] = pr_s[...].astype(BF16)
-    for i, peer in enumerate(y_peers):
-        remote(pr_send, pr_recv.at[i], p_sem.at[0], p_sem.at[1], peer)
+    @pl.when(core == 1)
+    def _():
+        wide_shape = (ROWS, both)
+        same_head = ((iota(wide_shape, 1) >> 2) & 3) == ((iota(wide_shape, 0) >> 2) & 3)
+        here = lane == zz * ROWS + iota(chunk, 0)
+
+        def column(row):
+            return jnp.sum(jnp.where(here, row, 0.0), axis=1, keepdims=True)
+
+        drafts = []
+        for c in (1, 0):
+            allowed = (dot(ancestors_of(c).astype(BF16), expand) > 0.5) & same_head
+            d_scores = nt_dot(qbuf[c * NX * NZ + slot], request_rows(kbuf, xx)) * factor
+            d_scores = jnp.where(allowed, d_scores, NEG)
+            d_peak = jnp.max(d_scores, axis=1, keepdims=True)
+            d_weights = jnp.where(allowed, jnp.exp(d_scores - d_peak), 0.0)
+            d_sum = jnp.sum(d_weights, axis=1, keepdims=True)
+            drafts.append((c, d_peak, d_sum, dot(d_weights.astype(BF16), request_rows(vbuf, xx))))
+        for c, d_peak, d_sum, d_out in drafts:
+            base = c * NX * NZ
+            arrived = pl.ds(base, NX * NZ)
+            wait(sbuf.at[arrived], s_sem.at[1 + c])
+            wait(obuf.at[arrived], o_sem.at[1 + c])
+            peaks = sbuf[arrived, :, :HEAD_DIM]
+            highest = jnp.max(peaks, axis=0)
+            shares = jnp.exp(peaks - highest[None])
+            sums = jnp.sum(shares * sbuf[arrived, :, HEAD_DIM:], axis=0)
+            top = column(highest)
+            merged = None
+            for s in range(NX * NZ):
+                part = column(shares[s]) * obuf[base + s].astype(F32)
+                merged = part if s == 0 else merged + part
+            best = jnp.maximum(top, d_peak)
+            c_share = jnp.exp(top - best)
+            d_share = jnp.exp(d_peak - best)
+            att_s[...] = (merged * c_share + d_out * d_share) / (column(sums) * c_share + d_sum * d_share)
+            att4 = [att_s[h * OWN : (h + 1) * OWN, :] for h in range(HEADS)]
+            att4 = jnp.concatenate(att4, axis=1).astype(BF16)
+            if c == 1:
+                c_wo.wait()
+            for n in range(NT):
+                pr_s[n * OWN : (n + 1) * OWN, :] = dot(att4, wo_s[:, n * WIDTH : (n + 1) * WIDTH])
+            pr_send[c] = pr_s[...].astype(BF16)
+            for i, peer in enumerate(y_peers):
+                remote(pr_send.at[c], pr_recv.at[i], p_sem.at[2 * c], p_sem.at[1], (peer[0] - 1 + c, peer[1]))
+            if c == 0:
+                remote(pr_send.at[0], pr_recv.at[NT - 1], p_sem.at[0], p_sem.at[1], partner)
+            else:
+                pr_recv[NT - 1] = pr_send[1]
+
+    @pl.when(core == 0)
+    def _():
+        c_wo.wait()
+
     for i, dx in enumerate((1, 3, 2)):
         compact(i + 1, dx)
     c_pg.wait()
-    wait(pr_recv, p_sem.at[1])
-    whole = pr_s[...] + pr_recv[0].astype(F32) + pr_recv[1].astype(F32) + pr_recv[2].astype(F32)
+
+    @pl.when(core == 0)
+    def _():
+        wait(pr_recv, p_sem.at[1])
+
+    @pl.when(core == 1)
+    def _():
+        wait(pr_recv.at[pl.ds(0, NT - 1)], p_sem.at[1])
+
+    whole = pr_recv[0].astype(F32) + pr_recv[1].astype(F32) + pr_recv[2].astype(F32) + pr_recv[3].astype(F32)
     pr_s[...] = whole
     quarters = [pr_s[n * OWN : (n + 1) * OWN, :] for n in range(NT)]
     squares = sum(part * part for part in quarters)
@@ -342,9 +397,20 @@
 
     wait(sq_recv.at[0], sq_sem.at[0])
     wait(sq_recv.at[1], sq_sem.at[2])
-    wait(kfull.at[:, mine, :], swap_sem.at[0])
-    wait(vfull.at[:, mine, :], swap_sem.at[2])
-    wait(qbuf.at[pl.ds(0, NX * NZ - 1)], q_send)
+    @pl.when(core == 0)
+    def _():
+        wait(kfull.at[:, first_block, :], swap_sem.at[0])
+        wait(vfull.at[:, first_block, :], swap_sem.at[2])
+        wait(qbuf.at[pl.ds(0, NX * NZ)], q_send)
+
+    @pl.when(core == 1)
+    def _():
+        wait(qbuf.at[pl.ds(0, NX * NZ - 1)], q_send)
+        wait(sbuf.at[pl.ds(0, 2 * (NX * NZ - 1))], s_sem.at[0])
+        wait(obuf.at[pl.ds(0, 2 * (NX * NZ - 1))], o_sem.at[0])
+        wait(pr_recv, p_sem.at[0])
+        wait(pr_recv.at[pl.ds(0, NT - 1)], p_sem.at[2])
+
     wait(kbuf.at[0, 0, pl.ds(0, NZ - 1)], z_sem.at[0])
     wait(vbuf.at[0, 0, pl.ds(0, NZ - 1)], z_sem.at[2])
     wait(kbuf.at[0, pl.ds(0, NX - 1)], x_sem.at[0])
@@ -352,9 +418,6 @@
     for i in range(NX):
         wait(kbuf.at[0, 0], c_sem.at[4 * i])
         wait(vbuf.at[0, 0], c_sem.at[4 * i + 2])
-    wait(sbuf.at[pl.ds(0, NX * NZ - 1)], s_sem.at[0])
-    wait(obuf.at[pl.ds(0, NX * NZ - 1)], o_sem.at[0])
-    wait(pr_recv, p_sem.at[0])
 
 
 def hand_out(a, b, c, out_a, out_b, out_c, sem):
@@ -382,14 +445,14 @@
         vmem((REQ, full, WIDTH), BF16), vmem((REQ, full, WIDTH), BF16), vmem((REQ, DRAFT, DRAFT), BF16),
         vmem((2, 8, HEAD_DIM), F32), vmem((2, NT - 1, 8, HEAD_DIM), F32),
         vmem((ROWS, HEAD_DIM), BF16), vmem((ROWS, HEAD_DIM), BF16), vmem((ROWS, HEAD_DIM), BF16),
-        vmem((NX * NZ, ROWS, HEAD_DIM), BF16),
+        vmem((NC * NX * NZ, ROWS, HEAD_DIM), BF16),
         vmem((NC, NX, NZ, ROWS, HEAD_DIM), BF16), vmem((NC, NX, NZ, ROWS, HEAD_DIM), BF16),
-        vmem((NX, NZ, ROWS, HEAD_DIM), BF16), vmem((NX, 1, 2 * HEAD_DIM), F32),
-        vmem((NX * NZ, ROWS, HEAD_DIM), BF16), vmem((NX * NZ, 1, 2 * HEAD_DIM), F32),
+        vmem((NC * NX, NZ, ROWS, HEAD_DIM), BF16), vmem((NC * NX, 1, 2 * HEAD_DIM), F32),
+        vmem((NC * NX * NZ, ROWS, HEAD_DIM), BF16), vmem((NC * NX * NZ, 1, 2 * HEAD_DIM), F32),
         vmem((ROWS, HEAD_DIM), F32), vmem((ROWS, WIDTH), F32),
-        vmem((ROWS, WIDTH), BF16), vmem((NT - 1, ROWS, WIDTH), BF16),
-        sems((14,)), sems((4,)), sems((4,)), sems((NX,)), sems, sems((4,)), sems((8,)), sems((16,)),
-        sems((2,)), sems((2,)), sems((2,)), pltpu.SemaphoreType.REGULAR,
+        vmem((NC, ROWS, WIDTH), BF16), vmem((NT, ROWS, WIDTH), BF16),
+        sems((14,)), sems((4,)), sems((4,)), sems((NC * NX,)), sems, sems((4,)), sems((8,)), sems((16,)),
+        sems((3,)), sems((3,)), sems((3,)), pltpu.SemaphoreType.REGULAR,
     ]
     anywhere = pl.BlockSpec(memory_space=pltpu.HBM)
     results = pl.pallas_call(

time: 31.7 us -> 31.2 us (0.984)
  the two profiles are of different devices: /device:TPU:6 before, /device:TPU:1 now
where the time goes in v4:
time: 31.2 us; the launch traced here: 31.1 us
  Pallas kernels  30.5 us (98%)
  between operations  0.64 us (2%)
    pallas_call x1, Pallas kernels, body(): pl.pallas_call(kernel, out_shape=(vmem((OWN, WIDTH), BF16), vmem(kc.shape...  29.5 us
    pallas_call x1, Pallas kernels, body(): pl.pallas_call(hand_out, out_shape=tuple((jax.ShapeDtypeStruct(part.shape...  1 us

profile of v4, /device:TPU:1, one launch (start us, length us, event | category | flops | bytes accessed | tf_op | source)
XLA Modules:
  0.0 31.1 jit_solution(10670872045559564843)
XLA Ops:
  0.6 29.5 %tree_attention.1 = (bf16[4,512]{1,0:T(4,128)(2,1)S(1)}, bf16[4,128,512]{2,1,0:T(8,128)(2,1)S(1)}, bf16[4,128,512]{2,1,0:T(8,128)(2,1)S(1)}) custom-call(bf16[4,2048]{1,0:T(4,128)(2,1)} %hid.1, bf16[2048,512]{1,0:T(8,128)(2,1)} %wq.1, bf16[2048,512]{1,0:T(8,128)(2,1)} %wk.1, bf16[2048,512]{1,0:T(8,128)(2,1)} %wv.1, bf16[512,2048]{1,0:T(8,128)(2,1)} %wo.1, ...), custom_call_target="tpu_custom_call" | custom-call | flops 300000000 | bytes 11000000 | tf_op jit(solution)/shard_map/tree_attention/pallas_call | solution.py:458
  30.1 1.0 %hand_out.1 = (bf16[4,512]{1,0:T(4,128)(2,1)}, bf16[4,128,512]{2,1,0:T(8,128)(2,1)}, bf16[4,128,512]{2,1,0:T(8,128)(2,1)}) custom-call(bf16[4,512]{1,0:T(4,128)(2,1)S(1)} %get-tuple-element.6.a, bf16[4,128,512]{2,1,0:T(8,128)(2,1)S(1)} %get-tuple-element.7.b, bf16[4,128,512]{2,1,0:T(8,128)(2,1)S(1)} %get-tuple-element.8.c), custom_call_target="tpu_custom_call" | custom-call | bytes 2200000 | tf_op jit(solution)/shard_map/hand_out/pallas_call | solution.py:473

commit v5 on v4

--- a/solution.py
+++ b/solution.py
@@ -238,7 +238,7 @@
         onward(vbuf, 3, 1, 4, 2)
         wait(kfull.at[:, first_block, :], swap_sem.at[1])
         wait(vfull.at[:, first_block, :], swap_sem.at[3])
-        for step, (c, dx) in enumerate([(c, dx) for c in (1, 0) for dx in PLANES]):
+        for step, (c, dx) in enumerate([(1, 0), (1, 1), (1, 3), (1, 2), (0, 2), (0, 1), (0, 3), (0, 0)]):
             if step == 2:
                 onward(kbuf, 1, 0, 1, 0)
             r = lax.rem(xx + dx, NX)

time: 31.2 us -> 30.7 us (0.984)
  Pallas kernels: 30.5 us -> 30 us
    pallas_call x1, Pallas kernels: 29.5 us -> 29 us  [body(): pl.pallas_call(kernel, out_shape=(vmem((OWN, WIDTH), BF16), vmem(kc.shape...]
where the time goes in v5:
time: 30.7 us; the launch traced here: 30.6 us
  Pallas kernels  30 us (98%)
  between operations  0.64 us (2%)
    pallas_call x1, Pallas kernels, body(): pl.pallas_call(kernel, out_shape=(vmem((OWN, WIDTH), BF16), vmem(kc.shape...  29 us
    pallas_call x1, Pallas kernels, body(): pl.pallas_call(hand_out, out_shape=tuple((jax.ShapeDtypeStruct(part.shape...  1 us

profile of v5, /device:TPU:1, one launch (start us, length us, event | category | flops | bytes accessed | tf_op | source)
XLA Modules:
  0.0 30.6 jit_solution(4304289739917354740)
XLA Ops:
  0.6 29.0 %tree_attention.1 = (bf16[4,512]{1,0:T(4,128)(2,1)S(1)}, bf16[4,128,512]{2,1,0:T(8,128)(2,1)S(1)}, bf16[4,128,512]{2,1,0:T(8,128)(2,1)S(1)}) custom-call(bf16[4,2048]{1,0:T(4,128)(2,1)} %hid.1, bf16[2048,512]{1,0:T(8,128)(2,1)} %wq.1, bf16[2048,512]{1,0:T(8,128)(2,1)} %wk.1, bf16[2048,512]{1,0:T(8,128)(2,1)} %wv.1, bf16[512,2048]{1,0:T(8,128)(2,1)} %wo.1, ...), custom_call_target="tpu_custom_call" | custom-call | flops 300000000 | bytes 11000000 | tf_op jit(solution)/shard_map/tree_attention/pallas_call | solution.py:458
  29.6 1.0 %hand_out.1 = (bf16[4,512]{1,0:T(4,128)(2,1)}, bf16[4,128,512]{2,1,0:T(8,128)(2,1)}, bf16[4,128,512]{2,1,0:T(8,128)(2,1)}) custom-call(bf16[4,512]{1,0:T(4,128)(2,1)S(1)} %get-tuple-element.6.a, bf16[4,128,512]{2,1,0:T(8,128)(2,1)S(1)} %get-tuple-element.7.b, bf16[4,128,512]{2,1,0:T(8,128)(2,1)S(1)} %get-tuple-element.8.c), custom_call_target="tpu_custom_call" | custom-call | bytes 2200000 | tf_op jit(solution)/shard_map/hand_out/pallas_call | solution.py:473

commit v6 on v5

--- a/solution.py
+++ b/solution.py
@@ -65,7 +65,7 @@
         return ((lax.rem(xx + dx, NX) * NZ + lax.rem(zz + dz, NZ)) * NC + on, tp)
 
     partner = (seq + 1 - 2 * core, tp)
-    y_peers = [(seq, lax.rem(tp + d, NT)) for d in range(1, NT)]
+    y_peers = [(seq, lax.rem(tp + d, NT)) for d in (2, 1, 3)]
     plane_peers = [at(a, b, 1) for a, b in far_first()]
     x_peers = [at(a, 0) for a in range(1, NX)]
     near_peers = [at(0, b) for b in range(1, NZ)] + x_peers + y_peers + [partner]
@@ -234,12 +234,15 @@
         tall = (NZ * ROWS, NC * BLOCK)
         tall_head = (iota(tall, 0) >> 2) & 3
         place = (seq - 1) * BLOCK + iota(tall, 1)
-        turn = iota((NZ * ROWS, HEAD_DIM), 0) == iota((NZ * ROWS, HEAD_DIM), 1)
+        half_rows = NZ * ROWS // 2
+        half_shape = (half_rows, HEAD_DIM)
+        peak_spot = iota(half_shape, 1) == iota(half_shape, 0)
+        sum_spot = iota(half_shape, 1) == iota(half_shape, 0) + half_rows
         onward(vbuf, 3, 1, 4, 2)
         wait(kfull.at[:, first_block, :], swap_sem.at[1])
         wait(vfull.at[:, first_block, :], swap_sem.at[3])
         for step, (c, dx) in enumerate([(1, 0), (1, 1), (1, 3), (1, 2), (0, 2), (0, 1), (0, 3), (0, 0)]):
-            if step == 2:
+            if step == 3:
                 onward(kbuf, 1, 0, 1, 0)
             r = lax.rem(xx + dx, NX)
             group = pl.ds((c * NX + r) * NZ, NZ)
@@ -260,16 +263,18 @@
                 part = dot(masked, vfull[r, :, h * HEAD_DIM : (h + 1) * HEAD_DIM])
                 mixed = part if h == 0 else mixed + part
             o_st[step] = mixed.astype(BF16).reshape(NZ, ROWS, HEAD_DIM)
-            s_st[step, :, :HEAD_DIM] = jnp.sum(jnp.where(turn, peak, 0.0), axis=0, keepdims=True)
-            s_st[step, :, HEAD_DIM:] = jnp.sum(jnp.where(turn, weight_sum, 0.0), axis=0, keepdims=True)
+            for n in range(2):
+                rows = slice(n * half_rows, (n + 1) * half_rows)
+                spots = jnp.where(peak_spot, peak[rows], jnp.where(sum_spot, weight_sum[rows], 0.0))
+                s_st[step, n] = jnp.sum(spots, axis=0, keepdims=True)
             there = c * NX * NZ + slot
             for dz in FAR_Z:
                 to = lax.rem(zz + dz, NZ)
                 if (dx, dz) == (0, 0):
                     pltpu.make_async_copy(o_st.at[step, to], obuf.at[there], o_sem.at[1 + c]).start()
-                    pltpu.make_async_copy(s_st.at[step], sbuf.at[there], s_sem.at[1 + c]).start()
+                    pltpu.make_async_copy(s_st.at[step, to // (NZ // 2)], sbuf.at[there], s_sem.at[1 + c]).start()
                 else:
-                    remote(s_st.at[step], sbuf.at[there], s_sem.at[0], s_sem.at[1 + c], at(dx, dz))
+                    remote(s_st.at[step, to // (NZ // 2)], sbuf.at[there], s_sem.at[0], s_sem.at[1 + c], at(dx, dz))
                     remote(o_st.at[step, to], obuf.at[there], o_sem.at[0], o_sem.at[1 + c], at(dx, dz))
 
     wait(kbuf.at[core, xx], c_sem.at[1])
@@ -321,7 +326,7 @@
     def _():
         wide_shape = (ROWS, both)
         same_head = ((iota(wide_shape, 1) >> 2) & 3) == ((iota(wide_shape, 0) >> 2) & 3)
-        here = lane == zz * ROWS + iota(chunk, 0)
+        here = lane == lax.rem(zz, NZ // 2) * ROWS + iota(chunk, 0)
 
         def column(row):
             return jnp.sum(jnp.where(here, row, 0.0), axis=1, keepdims=True)
@@ -340,10 +345,12 @@
             arrived = pl.ds(base, NX * NZ)
             wait(sbuf.at[arrived], s_sem.at[1 + c])
             wait(obuf.at[arrived], o_sem.at[1 + c])
-            peaks = sbuf[arrived, :, :HEAD_DIM]
-            highest = jnp.max(peaks, axis=0)
-            shares = jnp.exp(peaks - highest[None])
-            sums = jnp.sum(shares * sbuf[arrived, :, HEAD_DIM:], axis=0)
+            stats = sbuf[arrived]
+            highest = jnp.max(stats, axis=0)
+            shares = jnp.exp(stats - highest[None])
+            sums = shares[0] * pltpu.roll(stats[0], HEAD_DIM // 2, 1)
+            for s in range(1, NX * NZ):
+                sums = sums + shares[s] * pltpu.roll(stats[s], HEAD_DIM // 2, 1)
             top = column(highest)
             merged = None
             for s in range(NX * NZ):
@@ -447,8 +454,8 @@
         vmem((ROWS, HEAD_DIM), BF16), vmem((ROWS, HEAD_DIM), BF16), vmem((ROWS, HEAD_DIM), BF16),
         vmem((NC * NX * NZ, ROWS, HEAD_DIM), BF16),
         vmem((NC, NX, NZ, ROWS, HEAD_DIM), BF16), vmem((NC, NX, NZ, ROWS, HEAD_DIM), BF16),
-        vmem((NC * NX, NZ, ROWS, HEAD_DIM), BF16), vmem((NC * NX, 1, 2 * HEAD_DIM), F32),
-        vmem((NC * NX * NZ, ROWS, HEAD_DIM), BF16), vmem((NC * NX * NZ, 1, 2 * HEAD_DIM), F32),
+        vmem((NC * NX, NZ, ROWS, HEAD_DIM), BF16), vmem((NC * NX, 2, 1, HEAD_DIM), F32),
+        vmem((NC * NX * NZ, ROWS, HEAD_DIM), BF16), vmem((NC * NX * NZ, 1, HEAD_DIM), F32),
         vmem((ROWS, HEAD_DIM), F32), vmem((ROWS, WIDTH), F32),
         vmem((NC, ROWS, WIDTH), BF16), vmem((NT, ROWS, WIDTH), BF16),
         sems((14,)), sems((4,)), sems((4,)), sems((NC * NX,)), sems, sems((4,)), sems((8,)), sems((16,)),

time: 30.7 us -> 30.7 us (level)
  no operation moved by 1% of the time
where the time goes in v6:
time: 30.7 us
  Pallas kernels  30 us (98%)
  between operations  0.64 us (2%)
    pallas_call x1, Pallas kernels, body(): pl.pallas_call(kernel, out_shape=(vmem((OWN, WIDTH), BF16), vmem(kc.shape...  29 us
    pallas_call x1, Pallas kernels, body(): pl.pallas_call(hand_out, out_shape=tuple((jax.ShapeDtypeStruct(part.shape...  1 us

profile of v6, /device:TPU:1, one launch (start us, length us, event | category | flops | bytes accessed | tf_op | source)
XLA Modules:
  0.0 30.7 jit_solution(15322665800577279213)
XLA Ops:
  0.6 29.0 %tree_attention.1 = (bf16[4,512]{1,0:T(4,128)(2,1)S(1)}, bf16[4,128,512]{2,1,0:T(8,128)(2,1)S(1)}, bf16[4,128,512]{2,1,0:T(8,128)(2,1)S(1)}) custom-call(bf16[4,2048]{1,0:T(4,128)(2,1)} %hid.1, bf16[2048,512]{1,0:T(8,128)(2,1)} %wq.1, bf16[2048,512]{1,0:T(8,128)(2,1)} %wk.1, bf16[2048,512]{1,0:T(8,128)(2,1)} %wv.1, bf16[512,2048]{1,0:T(8,128)(2,1)} %wo.1, ...), custom_call_target="tpu_custom_call" | custom-call | flops 300000000 | bytes 11000000 | tf_op jit(solution)/shard_map/tree_attention/pallas_call | solution.py:465
  29.7 1.0 %hand_out.1 = (bf16[4,512]{1,0:T(4,128)(2,1)}, bf16[4,128,512]{2,1,0:T(8,128)(2,1)}, bf16[4,128,512]{2,1,0:T(8,128)(2,1)}) custom-call(bf16[4,512]{1,0:T(4,128)(2,1)S(1)} %get-tuple-element.6.a, bf16[4,128,512]{2,1,0:T(8,128)(2,1)S(1)} %get-tuple-element.7.b, bf16[4,128,512]{2,1,0:T(8,128)(2,1)S(1)} %get-tuple-element.8.c), custom_call_target="tpu_custom_call" | custom-call | bytes 2200000 | tf_op jit(solution)/shard_map/hand_out/pallas_call | solution.py:480
